TPU v7x, 128 devices: a whole 4x4x4 slice. The times are simulated.
128 devices in a mesh: gx: 16 (over z, y), gy: 8 (over x, core).
Axes of the slice: x: 4, y: 4, z: 4, core: 2. Of those that a mesh axis runs over, the one named last changes fastest.
Arguments:
- tokens_one: bfloat16 [32768, 768], P(('gx', 'gy')), may hold values from -6 to 6
- gates_one: float32 [32768], P(('gx', 'gy')), may hold values from 0.2 to 1
- routes_one: int32 [32768, 1], P(('gx', 'gy')), may hold values from 0 to 127; in each aligned block of 256 rows (0 to 255, 256 to 511, ...) at most 4 rows name the same one
- old_place: int32 [128], replicated, may hold values from 0 to 127, each once
- move_slots: int32 [25, 2], replicated, may hold values from 0 to 127, as said below
- tokens_two: bfloat16 [32768, 768], P(('gx', 'gy')), may hold values from -6 to 6
- gates_two: float32 [32768], P(('gx', 'gy')), may hold values from 0.2 to 1
- routes_two: int32 [32768, 1], P(('gx', 'gy')), may hold values from 0 to 127; in each aligned block of 256 rows (0 to 255, 256 to 511, ...) at most 4 rows name the same one
- expert_in: bfloat16 [128, 3072, 768], P(('gx', 'gy')), may hold values from -0.21875 to 0.21875
- expert_out: bfloat16 [128, 3072, 768], P(('gx', 'gy')), may hold values from -0.109375 to 0.109375
Outputs:
- mixed_one: bfloat16 [32768, 768], P(('gx', 'gy'))
- mixed_two: bfloat16 [32768, 768], P(('gx', 'gy'))
- expert_in_new: bfloat16 [128, 3072, 768], P(('gx', 'gy'))
- expert_out_new: bfloat16 [128, 3072, 768], P(('gx', 'gy'))
Inputs may be any that keep to these rules, and one draw needn't show every extreme that they name: `routes_one`: among the tokens of one device no expert is named by more than 4 tokens. `routes_two`: among the tokens of one device no slot is named by more than 4 tokens. `old_place`: each expert has one slot. `move_slots`: source slots lie on 25 distinct devices; the destination slots are the same set of slots, and no move stays on its device, so each device sends at most one expert and receives at most one.
All inputs are finite; a program needn't handle non-finite values.
Results may differ from a plain program's by a relative error of at most 0.0058.
Values may be sent and summed in bfloat16 or wider, within the bound.
A program may use at most 128 MiB of HBM per device.

v0:
```python
import jax
import jax.numpy as jnp
from jax import lax
from jax.sharding import PartitionSpec as P


def bucket_layout(slot_ids, total_slots, capacity):
    columns = jnp.arange(total_slots, dtype=jnp.int32)
    member = (slot_ids[:, None] == columns[None, :]).astype(jnp.int32)
    ranking = jnp.sum(jnp.cumsum(member, axis=0) * member, axis=1) - 1
    return slot_ids * capacity + ranking


def expert_block(received, weights_in, weights_out):
    hidden = jnp.einsum("semd,efd->semf", received, weights_in, preferred_element_type=jnp.float32)
    hidden = jnp.maximum(hidden, 0.0).astype(jnp.bfloat16)
    return jnp.einsum(
        "semf,efd->semd", hidden, weights_out, preferred_element_type=jnp.float32
    ).astype(jnp.bfloat16)


def run_batch(tokens, gates, slot_ids, weights_in, weights_out):
    width = tokens.shape[1]
    local_slots = weights_in.shape[0]
    grid_rows = lax.axis_size("gx")
    grid_cols = lax.axis_size("gy")
    device_count = grid_rows * grid_cols
    capacity = 2 * tokens.shape[0] // (local_slots * device_count)
    layout = bucket_layout(slot_ids, local_slots * device_count, capacity)
    outbox = (
        jnp.zeros((local_slots * device_count * capacity, width), jnp.bfloat16)
        .at[layout]
        .set(tokens)
    )
    framed = outbox.reshape(device_count, local_slots, capacity, width)
    produced = expert_block(
        lax.all_to_all(framed, ("gx", "gy"), split_axis=0, concat_axis=0, tiled=True),
        weights_in,
        weights_out,
    )
    returned = lax.all_to_all(produced, ("gx", "gy"), split_axis=0, concat_axis=0, tiled=True)
    gathered = returned.reshape(-1, width)[layout]
    return (gates[:, None] * gathered.astype(jnp.float32)).astype(jnp.bfloat16)


def relocate(expert_in, expert_out, move_slots):
    local_slots = expert_in.shape[0]
    hidden_units = expert_in.shape[1]
    width = expert_in.shape[2]
    grid_rows = lax.axis_size("gx")
    grid_cols = lax.axis_size("gy")
    device_count = grid_rows * grid_cols
    myself = lax.axis_index(("gx", "gy"))
    sources = move_slots[:, 0]
    targets = move_slots[:, 1]
    leaving = sources // local_slots == myself
    leave_slot = jnp.sum(jnp.where(leaving, sources % local_slots, 0))
    depart_in = lax.dynamic_index_in_dim(expert_in, leave_slot, 0, keepdims=False)
    depart_out = lax.dynamic_index_in_dim(expert_out, leave_slot, 0, keepdims=False)
    block_rows = hidden_units // device_count
    devices = jnp.arange(device_count, dtype=jnp.int32)
    landing = (targets // local_slots)[None, :] == devices[:, None]
    anchor = jnp.sum(jnp.where(landing, (sources // local_slots)[None, :], 0), axis=1)
    flat_shape = (device_count, block_rows, width)
    held_in, held_out = (
        lax.all_to_all(
            depart_in.reshape(flat_shape), ("gx", "gy"), split_axis=0, concat_axis=0, tiled=True
        ),
        lax.all_to_all(
            depart_out.reshape(flat_shape), ("gx", "gy"), split_axis=0, concat_axis=0, tiled=True
        ),
    )
    forward_in = jnp.take(held_in, anchor, axis=0)
    forward_out = jnp.take(held_out, anchor, axis=0)
    arrived_in, arrived_out = (
        lax.all_to_all(forward_in, ("gx", "gy"), split_axis=0, concat_axis=0, tiled=True),
        lax.all_to_all(forward_out, ("gx", "gy"), split_axis=0, concat_axis=0, tiled=True),
    )
    arriving = targets // local_slots == myself
    arrive_slot = jnp.sum(jnp.where(arriving, targets % local_slots, 0))
    replace = (jnp.arange(local_slots, dtype=jnp.int32) == arrive_slot) & jnp.any(arriving)
    replace = replace[:, None, None]
    fresh_in = jnp.where(replace, arrived_in.reshape(1, hidden_units, width), expert_in)
    fresh_out = jnp.where(replace, arrived_out.reshape(1, hidden_units, width), expert_out)
    return (fresh_in, fresh_out)


def shards(
    tokens_one,
    gates_one,
    routes_one,
    old_place,
    move_slots,
    tokens_two,
    gates_two,
    routes_two,
    expert_in,
    expert_out,
):
    experts_all = old_place.shape[0]
    columns = jnp.arange(experts_all, dtype=jnp.int32)
    member = routes_one[:, 0][:, None] == columns[None, :]
    slot_one = jnp.sum(jnp.where(member, old_place[None, :], 0), axis=1)
    mixed_one = run_batch(tokens_one, gates_one, slot_one, expert_in, expert_out)
    target = routes_two[:, 0]
    fresh_in, fresh_out = relocate(expert_in, expert_out, move_slots)
    mixed_two = run_batch(tokens_two, gates_two, target, fresh_in, fresh_out)
    return (mixed_one, mixed_two, fresh_in, fresh_out)


def solution(mesh):
    return jax.shard_map(
        shards,
        mesh=mesh,
        in_specs=(
            P(("gx", "gy"), None),
            P(("gx", "gy")),
            P(("gx", "gy"), None),
            P(),
            P(),
            P(("gx", "gy"), None),
            P(("gx", "gy")),
            P(("gx", "gy"), None),
            P(("gx", "gy"), None, None),
            P(("gx", "gy"), None, None),
        ),
        out_specs=(
            P(("gx", "gy"), None),
            P(("gx", "gy"), None),
            P(("gx", "gy"), None, None),
            P(("gx", "gy"), None, None),
        ),
        check_vma=False,
    )
```

profile of v0, /device:TPU:1, one launch (start us, length us, event | category | flops | bytes accessed | tf_op | source)
XLA Modules:
  0.0 356.3 jit_solution(12821963732499423611)
XLA Ops:
  0.6 70.3 %all_to_all.40 = bf16[128,24,768]{2,1,0:T(8,128)(2,1)} all-to-all(bf16[128,24,768]{2,1,0:T(8,128)(2,1)} %bitcast.104), channel_id=1, replica_groups=mesh['gx'=16,'gy'=8] {'gx','gy'}, dimensions={0} | all-to-all | bytes 9437184 | tf_op jit(solution)/shard_map/all_to_all | solution.py:69
  70.9 5.5 %all-to-all-start.4 = ((bf16[128,24,768]{2,1,0:T(8,128)(2,1)}), bf16[128,24,768]{2,1,0:T(8,128)(2,1)}, u32[]{:S(2)}, u32[]{:S(2)}) async-start(bf16[128,24,768]{2,1,0:T(8,128)(2,1)} %bitcast.103), calls=%async_computation.4 | async-start | bytes 9437184 | tf_op jit(solution)/shard_map/all_to_all | solution.py:66
  76.8 0.2 fusion.37
  77.3 2.3 scatter_custom_fusion
  79.6 1.1 reshape.158
  80.8 54.0 %all-to-all-done.4 = bf16[128,24,768]{2,1,0:T(8,128)(2,1)} async-done(((bf16[128,24,768]{2,1,0:T(8,128)(2,1)}), bf16[128,24,768]{2,1,0:T(8,128)(2,1)}, u32[]{:S(2)}, u32[]{:S(2)}) %all-to-all-start.4) | async-done | bytes 4718624 | tf_op jit(solution)/shard_map/all_to_all | solution.py:66
  134.8 4.4 %all-to-all-start = ((bf16[128,1,4,768]{3,2,1,0:T(4,128)(2,1)}), bf16[128,1,4,768]{3,2,1,0:T(4,128)(2,1)S(1)}, u32[]{:S(2)}, u32[]{:S(2)}) async-start(bf16[128,1,4,768]{3,2,1,0:T(4,128)(2,1)} %bitcast.7), calls=%async_computation | async-start | bytes 1572864 | tf_op jit(solution)/shard_map/all_to_all | solution.py:37
  139.3 5.4 %gather_fusion.2 = bf16[128,24,768]{2,1,0:T(8,128)(2,1)} fusion(bf16[128,24,768]{2,1,0:T(8,128)(2,1)} %all_to_all.40, s32[1024]{0:T(1024)S(1)} %pad_clamp_fusion.1), kind=kCustom, calls=%fused_computation.clone | custom fusion | bytes 9437696 | tf_op jit(solution)/shard_map/jit(_take)/gather | solution.py:74
  144.6 5.4 %gather_fusion.3 = bf16[128,24,768]{2,1,0:T(8,128)(2,1)} fusion(bf16[128,24,768]{2,1,0:T(8,128)(2,1)} %all-to-all-done.4, s32[1024]{0:T(1024)S(1)} %pad_clamp_fusion.1), kind=kCustom, calls=%fused_computation.1.clone | custom fusion | bytes 9437696 | tf_op jit(solution)/shard_map/jit(_take)/gather | solution.py:73
  150.0 8.4 %broadcast_select_fusion = (bf16[128,24,768]{2,1,0:T(8,128)(2,1)}, bf16[128,24,768]{2,1,0:T(8,128)(2,1)}) fusion(bf16[128,24,768]{2,1,0:T(8,128)(2,1)} %gather_fusion.3, pred[128]{0:T(512)(128)(4,1)S(1)} %compare_and_fusion, bf16[128,24,768]{2,1,0:T(8,128)(2,1)} %gather_fusion.2), kind=kLoop, calls=%fused_computation.16 | loop fusion | flops 4718592 | bytes 18874496 | tf_op jit(solution)/shard_map/jit(_take)/select_n | solution.py:73
  158.4 68.7 %all_to_all.41 = bf16[128,24,768]{2,1,0:T(8,128)(2,1)} all-to-all(bf16[128,24,768]{2,1,0:T(8,128)(2,1)} %get-tuple-element.7), channel_id=1, replica_groups=mesh['gx'=16,'gy'=8] {'gx','gy'}, dimensions={0} | all-to-all | bytes 9437184 | tf_op jit(solution)/shard_map/all_to_all | solution.py:76
  227.1 5.5 %all-to-all-start.3 = ((bf16[128,24,768]{2,1,0:T(8,128)(2,1)}), bf16[128,24,768]{2,1,0:T(8,128)(2,1)}, u32[]{:S(2)}, u32[]{:S(2)}) async-start(bf16[128,24,768]{2,1,0:T(8,128)(2,1)} %get-tuple-element.8), calls=%async_computation.3 | async-start | bytes 9437184 | tf_op jit(solution)/shard_map/all_to_all | solution.py:77
  233.3 2.5 scatter_custom_fusion.1
  235.8 1.1 reshape.170
  236.9 0.6 compare_reduce_fusion
  237.5 9.0 %fusion.20 = bf16[128,1,4,768]{3,0,2,1:T(8,128)(2,1)S(1)} fusion(bf16[1,3072,768]{2,1,0:T(8,128)(2,1)} %param.21, bf16[1,3072,768]{2,1,0:T(8,128)(2,1)} %param.20, bf16[128,1,4,768]{3,2,1,0:T(4,128)(2,1)S(1)} %all-to-all-done), kind=kOutput, calls=%fused_computation.22 | convolution fusion | flops 4835377152 | bytes 11010048 | tf_op jit(solution)/shard_map/semf,efd->semd/dot_general | solution.py:17
  246.5 1.5 copy.42
  248.0 5.7 %bitcast_select_fusion = bf16[1,3072,768]{2,1,0:T(8,128)(2,1)} fusion(bf16[1,3072,768]{2,1,0:T(8,128)(2,1)} %param.20, pred[]{:T(512)} %compare_reduce_fusion, bf16[1,3072,768]{2,1,0:T(8,128)(2,1)} %bitcast.105), kind=kLoop, calls=%fused_computation.11 | loop fusion | flops 2359296 | bytes 14155777 | tf_op jit(solution)/shard_map/jit(_where)/select_n | solution.py:83
  253.7 37.3 %all-to-all-done.3 = bf16[128,24,768]{2,1,0:T(8,128)(2,1)} async-done(((bf16[128,24,768]{2,1,0:T(8,128)(2,1)}), bf16[128,24,768]{2,1,0:T(8,128)(2,1)}, u32[]{:S(2)}, u32[]{:S(2)}) %all-to-all-start.3) | async-done | bytes 4718624 | tf_op jit(solution)/shard_map/all_to_all | solution.py:77
  291.0 4.4 %all-to-all-start.6 = ((bf16[128,1,4,768]{3,2,1,0:T(4,128)(2,1)}), bf16[128,1,4,768]{3,2,1,0:T(4,128)(2,1)S(1)}, u32[]{:S(2)}, u32[]{:S(2)}) async-start(bf16[128,1,4,768]{3,2,1,0:T(4,128)(2,1)} %bitcast.33), calls=%async_computation.6 | async-start | bytes 1572864 | tf_op jit(solution)/shard_map/all_to_all | solution.py:37
  295.5 5.7 %bitcast_select_fusion.1 = bf16[1,3072,768]{2,1,0:T(8,128)(2,1)} fusion(bf16[1,3072,768]{2,1,0:T(8,128)(2,1)} %param.21, pred[]{:T(512)} %compare_reduce_fusion, bf16[1,3072,768]{2,1,0:T(8,128)(2,1)} %bitcast.96), kind=kLoop, calls=%fused_computation.12 | loop fusion | flops 2359296 | bytes 14155777 | tf_op jit(solution)/shard_map/jit(_where)/select_n | solution.py:84
  301.1 11.0 %all-to-all-done.6 = bf16[128,1,4,768]{3,2,1,0:T(4,128)(2,1)S(1)} async-done(((bf16[128,1,4,768]{3,2,1,0:T(4,128)(2,1)}), bf16[128,1,4,768]{3,2,1,0:T(4,128)(2,1)S(1)}, u32[]{:S(2)}, u32[]{:S(2)}) %all-to-all-start.6) | async-done | bytes 786464 | tf_op jit(solution)/shard_map/all_to_all | solution.py:37
  312.1 4.4 %all-to-all-start.1 = ((bf16[128,1,4,768]{3,2,1,0:T(4,128)(2,1)}), bf16[128,1,4,768]{3,2,1,0:T(4,128)(2,1)S(1)}, u32[]{:S(2)}, u32[]{:S(2)}) async-start(bf16[128,1,4,768]{3,2,1,0:T(4,128)(2,1)} %copy.42), calls=%async_computation.1 | async-start | bytes 1572864 | tf_op jit(solution)/shard_map/all_to_all | solution.py:41
  316.6 8.9 %fusion.15 = bf16[128,1,4,768]{0,3,2,1:T(8,128)(2,1)S(1)} fusion(bf16[1,3072,768]{2,1,0:T(8,128)(2,1)} %bitcast_select_fusion.1, bf16[1,3072,768]{2,1,0:T(8,128)(2,1)} %bitcast_select_fusion, bf16[128,1,4,768]{3,2,1,0:T(4,128)(2,1)S(1)} %all-to-all-done.6), kind=kOutput, calls=%fused_computation.21 | convolution fusion | flops 4835377152 | bytes 11010048 | tf_op jit(solution)/shard_map/semf,efd->semd/dot_general | solution.py:17
  325.4 1.3 copy.49
  326.7 6.4 %all-to-all-done.1 = bf16[128,1,4,768]{3,2,1,0:T(4,128)(2,1)S(1)} async-done(((bf16[128,1,4,768]{3,2,1,0:T(4,128)(2,1)}), bf16[128,1,4,768]{3,2,1,0:T(4,128)(2,1)S(1)}, u32[]{:S(2)}, u32[]{:S(2)}) %all-to-all-start.1) | async-done | bytes 786464 | tf_op jit(solution)/shard_map/all_to_all | solution.py:41
  333.1 4.4 %all-to-all-start.7 = ((bf16[128,1,4,768]{3,2,1,0:T(4,128)(2,1)}), bf16[128,1,4,768]{3,2,1,0:T(4,128)(2,1)S(1)}, u32[]{:S(2)}, u32[]{:S(2)}) async-start(bf16[128,1,4,768]{3,2,1,0:T(4,128)(2,1)} %copy.49), calls=%async_computation.7 | async-start | bytes 1572864 | tf_op jit(solution)/shard_map/all_to_all | solution.py:41
  337.8 1.2 gather_fusion
  339.0 0.9 multiply_convert_fusion.1
  339.8 14.2 %all-to-all-done.7 = bf16[128,1,4,768]{3,2,1,0:T(4,128)(2,1)S(1)} async-done(((bf16[128,1,4,768]{3,2,1,0:T(4,128)(2,1)}), bf16[128,1,4,768]{3,2,1,0:T(4,128)(2,1)S(1)}, u32[]{:S(2)}, u32[]{:S(2)}) %all-to-all-start.7) | async-done | bytes 786464 | tf_op jit(solution)/shard_map/all_to_all | solution.py:41
  354.3 1.2 gather_fusion.1
  355.5 0.9 multiply_convert_fusion
  (44 shorter events, 1.7 us)
Async XLA Ops:
  70.9 5.5 %copy-start.3 = (s32[256,1]{0,1:T(1,128)S(1)}, s32[256,1]{0,1:T(1,128)}, u32[]{:S(2)}) copy-start(s32[256,1]{0,1:T(1,128)} %param.14) | copy-start | bytes 3076
  70.9 5.5 %copy-start.5 = (s32[128]{0:T(128)S(1)}, s32[128]{0:T(128)}, u32[]{:S(2)}) copy-start(s32[128]{0:T(128)} %param.15) | copy-start | bytes 1540
  70.9 9.8 %copy-start.4 = (s32[25,2]{0,1:T(2,128)S(1)}, s32[25,2]{0,1:T(2,128)}, u32[]{:S(2)}) copy-start(s32[25,2]{0,1:T(2,128)} %param.16) | copy-start | bytes 604
  70.9 63.9 %all-to-all-start.4 = ((bf16[128,24,768]{2,1,0:T(8,128)(2,1)}), bf16[128,24,768]{2,1,0:T(8,128)(2,1)}, u32[]{:S(2)}, u32[]{:S(2)}) async-start(bf16[128,24,768]{2,1,0:T(8,128)(2,1)} %bitcast.103), calls=%async_computation.4 | async-start | bytes 9437184 | tf_op jit(solution)/shard_map/all_to_all | solution.py:66
  134.8 23.6 %all-to-all-start = ((bf16[128,1,4,768]{3,2,1,0:T(4,128)(2,1)}), bf16[128,1,4,768]{3,2,1,0:T(4,128)(2,1)S(1)}, u32[]{:S(2)}, u32[]{:S(2)}) async-start(bf16[128,1,4,768]{3,2,1,0:T(4,128)(2,1)} %bitcast.7), calls=%async_computation | async-start | bytes 1572864 | tf_op jit(solution)/shard_map/all_to_all | solution.py:37
  227.1 5.5 %copy-start = (s32[256,1]{0,1:T(1,128)S(1)}, s32[256,1]{0,1:T(1,128)}, u32[]{:S(2)}) copy-start(s32[256,1]{0,1:T(1,128)} %param.19) | copy-start | bytes 3076
  227.1 63.9 %all-to-all-start.3 = ((bf16[128,24,768]{2,1,0:T(8,128)(2,1)}), bf16[128,24,768]{2,1,0:T(8,128)(2,1)}, u32[]{:S(2)}, u32[]{:S(2)}) async-start(bf16[128,24,768]{2,1,0:T(8,128)(2,1)} %get-tuple-element.8), calls=%async_computation.3 | async-start | bytes 9437184 | tf_op jit(solution)/shard_map/all_to_all | solution.py:77
  291.0 21.1 %all-to-all-start.6 = ((bf16[128,1,4,768]{3,2,1,0:T(4,128)(2,1)}), bf16[128,1,4,768]{3,2,1,0:T(4,128)(2,1)S(1)}, u32[]{:S(2)}, u32[]{:S(2)}) async-start(bf16[128,1,4,768]{3,2,1,0:T(4,128)(2,1)} %bitcast.33), calls=%async_computation.6 | async-start | bytes 1572864 | tf_op jit(solution)/shard_map/all_to_all | solution.py:37
  312.1 21.0 %all-to-all-start.1 = ((bf16[128,1,4,768]{3,2,1,0:T(4,128)(2,1)}), bf16[128,1,4,768]{3,2,1,0:T(4,128)(2,1)S(1)}, u32[]{:S(2)}, u32[]{:S(2)}) async-start(bf16[128,1,4,768]{3,2,1,0:T(4,128)(2,1)} %copy.42), calls=%async_computation.1 | async-start | bytes 1572864 | tf_op jit(solution)/shard_map/all_to_all | solution.py:41
  325.4 13.5 %copy-start.1 = (f32[256]{0:T(256)S(1)}, f32[256]{0:T(256)}, u32[]{:S(2)}) copy-start(f32[256]{0:T(256)} %param.13) | copy-start | bytes 3076
  333.1 21.0 %all-to-all-start.7 = ((bf16[128,1,4,768]{3,2,1,0:T(4,128)(2,1)}), bf16[128,1,4,768]{3,2,1,0:T(4,128)(2,1)S(1)}, u32[]{:S(2)}, u32[]{:S(2)}) async-start(bf16[128,1,4,768]{3,2,1,0:T(4,128)(2,1)} %copy.49), calls=%async_computation.7 | async-start | bytes 1572864 | tf_op jit(solution)/shard_map/all_to_all | solution.py:41
  337.7 17.7 %copy-start.2 = (f32[256]{0:T(256)S(1)}, f32[256]{0:T(256)}, u32[]{:S(2)}) copy-start(f32[256]{0:T(256)} %param.18) | copy-start | bytes 3076
where the time goes:
time: 357 us; the launch traced here: 356 us
  blocking collectives  139 us (39%)
  waiting for transfers between devices  123 us (34%)
  starting transfers between devices  28.7 us (8%)
  local copies, waits for them, and re-layouts  23.6 us (7%)
  other arithmetic  23.3 us (7%)
  matrix products  17.8 us (5%)
    all_to_all x1, blocking collectives, relocate(): lax.all_to_all(depart_out.reshape(flat_shape), ('gx', 'gy'), split_axis=0...  70.3 us
    all_to_all x1, blocking collectives, relocate(): lax.all_to_all(forward_in, ('gx', 'gy'), split_axis=0, concat_axis=0, til...  68.7 us
    all_to_all x1, waiting for transfers between devices, relocate(): lax.all_to_all(depart_in.reshape(flat_shape), ('gx', 'gy'), split_axis=0,...  54 us
    all_to_all x1, waiting for transfers between devices, relocate(): lax.all_to_all(forward_out, ('gx', 'gy'), split_axis=0, concat_axis=0, ti...  37.3 us
    all_to_all x2, waiting for transfers between devices, run_batch(): lax.all_to_all(produced, ('gx', 'gy'), split_axis=0, concat_axis=0, tiled...  20.6 us
    dot_general x2, matrix products, expert_block(): jnp.einsum('semf,efd->semd', hidden, weights_out, preferred_element_type=...  17.8 us
    all_to_all x2, waiting for transfers between devices, run_batch(): lax.all_to_all(framed, ('gx', 'gy'), split_axis=0, concat_axis=0, tiled=T...  11 us
    all_to_all x2, starting transfers between devices, run_batch(): lax.all_to_all(framed, ('gx', 'gy'), split_axis=0, concat_axis=0, tiled=T...  8.87 us
  transfers between devices with their start and end apart: 6, of which 5 were waited for; matrix products, arithmetic and copies ran while one was open for 18% of the time, Pallas kernels for 0%

commit v1 on v0

v1 whole, which is shorter than its diff:
```python
import functools

import jax
import jax.numpy as jnp
from jax import lax
from jax.experimental import pallas as pl
from jax.experimental.pallas import tpu as pltpu
from jax.sharding import PartitionSpec as P

MESH = pl.DeviceIdType.MESH
SIDE = 4
CORES = 2
LINE = SIDE * CORES
TURNS = ((0, 1, 2), (1, 2, 0), (2, 0, 1))
LINE_MOST = 5
PLANE_MOST = 6


def bucket_layout(slot_ids, total_slots):
    columns = jnp.arange(total_slots, dtype=jnp.int32)
    member = (slot_ids[:, None] == columns[None, :]).astype(jnp.int32)
    return jnp.sum(jnp.cumsum(member, axis=0) * member, axis=1) - 1


def coordinates(device):
    return ((device // CORES) % SIDE, (device // LINE) % SIDE, device // (LINE * SIDE)), device % CORES


def mesh_id(place, core):
    x, y, z = place
    return (z * SIDE + y, x * CORES + core)


def plan_tables(move_slots, myself):
    moves = move_slots.shape[0]
    source, target = move_slots[:, 0], move_slots[:, 1]
    s_at, s_core = coordinates(source)
    t_at, t_core = coordinates(target)
    m_at, m_core = coordinates(myself)
    order = jnp.arange(moves, dtype=jnp.int32)

    def stack(at, axis):
        return jnp.stack([at[turn[axis]] for turn in TURNS])

    sa, sb, sc = (stack(s_at, axis) for axis in range(3))
    ta, tb, tc = (stack(t_at, axis) for axis in range(3))
    ma, mb, mc = (stack(m_at, axis) for axis in range(3))
    s_line, t_line, planes = sb * SIDE + sc, tb * SIDE + tc, sc * SIDE + tc
    m_line = mb * SIDE + mc

    def rank(group):
        return jnp.sum(
            (group[:, :, None] == group[:, None, :]) & (order[None, :] < order[:, None]),
            axis=2,
            dtype=jnp.int32,
        )

    rank_s, rank_p, rank_t = rank(s_line), rank(planes), rank(t_line)
    fits = (
        (jnp.max(rank_s) < LINE_MOST) & (jnp.max(rank_t) < LINE_MOST) & (jnp.max(rank_p) < PLANE_MOST)
    )

    def pick(mask, slot, count, value):
        hit = mask[:, None, :] & (slot[:, None, :] == jnp.arange(count, dtype=jnp.int32)[None, :, None])
        return jnp.sum(jnp.where(hit, value[:, None, :], 0), axis=2, dtype=jnp.int32)

    two = pick(s_line == m_line[:, None], rank_s, LINE_MOST, sa * CORES + s_core[None])
    three = pick(
        (sc == mc[:, None]) & (rank_p < PLANE_MOST),
        tc * PLANE_MOST + rank_p,
        SIDE * PLANE_MOST,
        jnp.minimum(sb * LINE_MOST + rank_s, SIDE * LINE_MOST - 1),
    )
    four = pick(
        (tc == mc[:, None]) & (rank_t < LINE_MOST),
        tb * LINE_MOST + rank_t,
        SIDE * LINE_MOST,
        jnp.minimum(sc * PLANE_MOST + rank_p, SIDE * PLANE_MOST - 1),
    )
    five = pick(
        t_line == m_line[:, None], ta * CORES + t_core[None], LINE, jnp.minimum(rank_t, LINE_MOST - 1)
    )
    return two, three, four, five, fits


def relocate_kernel(
    two, three, four, five, w_in, w_out, new_in, new_out, first, sent, spread, crossing, crossed, landed, local, send, recv
):
    gx, gy = lax.axis_index("gx"), lax.axis_index("gy")
    at, core = (gy // CORES, gx % SIDE, gx // SIDE), gy % CORES
    piece = first[0][0].shape[1]
    block = spread[0][0].shape[2]
    third = piece * LINE
    sources, targets = (w_in, w_out), (new_in, new_out)
    others = [(step, flip) for step in range(SIDE) for flip in range(CORES) if (step, flip) != (0, 0)]

    def beside(axis, step, flip=0):
        place = list(at)
        place[axis] = (place[axis] + step) % SIDE
        return place, (core + flip) % CORES

    barrier = pltpu.get_barrier_semaphore()
    peers = [beside(0, 0, 1)] + [
        beside(axis, step, flip) for axis in range(3) for step in range(1, SIDE) for flip in range(CORES)
    ]
    for place, which in peers:
        pl.semaphore_signal(barrier, inc=1, device_id=mesh_id(place, which), device_id_type=MESH)
    pl.semaphore_wait(barrier, len(peers))

    def ship(src, dst, stage, half, turn, place, which):
        pltpu.make_async_remote_copy(
            src_ref=src,
            dst_ref=dst,
            send_sem=send.at[stage, half, turn],
            recv_sem=recv.at[stage, half, turn],
            device_id=mesh_id(place, which),
            device_id_type=MESH,
        ).start()

    def settle(semaphore, ref):
        pltpu.make_async_copy(ref, ref, semaphore).wait()

    def rows(turn, index):
        return pl.ds(pl.multiple_of(turn * third + index * piece, piece), piece)

    def spot(turn):
        return at[TURNS[turn][0]] * CORES + core

    def own_first(half, turn):
        me = spot(turn)
        return pltpu.make_async_copy(
            sources[half].at[rows(turn, me)], first[half][turn].at[me], local.at[0, half, turn]
        )

    def own_last(half, turn):
        me = spot(turn)
        return pltpu.make_async_copy(
            first[half][turn].at[me], targets[half].at[rows(turn, me)], local.at[1, half, turn]
        )

    def stage_one(half):
        for turn in range(3):
            me = spot(turn)
            for step, flip in others:
                place, which = beside(TURNS[turn][0], step, flip)
                index = place[TURNS[turn][0]] * CORES + which
                ship(
                    sources[half].at[rows(turn, index)], first[half][turn].at[me], 0, half, turn, place, which
                )
            own_first(half, turn).start()

    def stage_two(half):
        for turn in range(3):
            b = TURNS[turn][1]
            own_first(half, turn).wait()
            settle(recv.at[0, half, turn], first[half][turn].at[pl.ds(0, LINE - 1)])
            for step in (1, 2, 3, 0):
                place, which = beside(b, step)
                cut = pl.ds(pl.multiple_of(place[b] * block, block), block)

                def take(k, carry):
                    data = first[half][turn][two[turn, k], cut, :]
                    if step == 0:
                        spread[half][turn][at[b], k] = data
                    else:
                        sent[half, turn, step - 1, k] = data
                    return carry

                lax.fori_loop(0, LINE_MOST, take, 0)
                if step:
                    ship(sent.at[half, turn, step - 1], spread[half][turn].at[at[b]], 1, half, turn, place, which)

    def stage_three(half):
        for turn in range(3):
            c = TURNS[turn][2]
            settle(recv.at[1, half, turn], spread[half][turn].at[pl.ds(0, SIDE - 1)])
            for step in (1, 2, 3, 0):
                place, which = beside(c, step)

                def take(k, carry):
                    index = three[turn, place[c] * PLANE_MOST + k]
                    data = spread[half][turn][index // LINE_MOST, index % LINE_MOST]
                    if step == 0:
                        crossed[half][turn][at[c], k] = data
                    else:
                        crossing[half, turn, step - 1, k] = data
                    return carry

                lax.fori_loop(0, PLANE_MOST, take, 0)
                if step:
                    ship(crossing.at[half, turn, step - 1], crossed[half][turn].at[at[c]], 2, half, turn, place, which)

    def stage_four(half):
        for turn in range(3):
            b = TURNS[turn][1]
            settle(recv.at[2, half, turn], crossed[half][turn].at[pl.ds(0, SIDE - 1)])
            settle(send.at[1, half, turn], sent.at[half, turn])
            for step in (1, 2, 3, 0):
                place, which = beside(b, step)

                def take(k, carry):
                    index = four[turn, place[b] * LINE_MOST + k]
                    data = crossed[half][turn][index // PLANE_MOST, index % PLANE_MOST]
                    if step == 0:
                        landed[half][turn][at[b], k] = data
                    else:
                        sent[half, turn, step - 1, k] = data
                    return carry

                lax.fori_loop(0, LINE_MOST, take, 0)
                if step:
                    ship(sent.at[half, turn, step - 1], landed[half][turn].at[at[b]], 3, half, turn, place, which)

    def stage_five(half):
        for turn in range(3):
            me = spot(turn)
            settle(recv.at[3, half, turn], landed[half][turn].at[pl.ds(0, SIDE - 1)])
            for step, flip in others + [(0, 0)]:
                place, which = beside(TURNS[turn][0], step, flip)
                index = place[TURNS[turn][0]] * CORES + which
                chosen = five[turn, index]

                def take(quarter, carry):
                    first[half][turn][index, pl.ds(pl.multiple_of(quarter * block, block), block), :] = landed[half][turn][
                        quarter, chosen
                    ]
                    return carry

                lax.fori_loop(0, SIDE, take, 0)
                if (step, flip) != (0, 0):
                    ship(
                        first[half][turn].at[index], targets[half].at[rows(turn, me)], 4, half, turn, place, which
                    )
            own_last(half, turn).start()

    for stage in (stage_one, stage_two, stage_three, stage_four, stage_five):
        for half in range(2):
            stage(half)

    for half in range(2):
        for turn in range(3):
            settle(send.at[0, half, turn], first[half][turn].at[pl.ds(0, LINE - 1)])
            settle(send.at[2, half, turn], crossing.at[half, turn])
            settle(send.at[3, half, turn], sent.at[half, turn])
            settle(send.at[4, half, turn], first[half][turn].at[pl.ds(0, LINE - 1)])
            settle(recv.at[4, half, turn], targets[half].at[pl.ds(0, (LINE - 1) * piece)])
            own_last(half, turn).wait()


def relocate_lines(expert_in, expert_out, two, three, four, five):
    hidden_units, width = expert_in.shape
    piece = hidden_units // (3 * LINE)
    block = piece // SIDE
    dtype = expert_in.dtype
    smem = pl.BlockSpec(memory_space=pltpu.SMEM)
    hbm = pl.BlockSpec(memory_space=pl.ANY)

    def each(*shape):
        return [[pltpu.VMEM(shape, dtype)] * 3] * 2

    return pl.pallas_call(
        relocate_kernel,
        out_shape=[jax.ShapeDtypeStruct((hidden_units, width), dtype)] * 2,
        in_specs=[smem] * 4 + [hbm] * 2,
        out_specs=[hbm] * 2,
        scratch_shapes=[
            each(LINE, piece, width),
            pltpu.VMEM((2, 3, SIDE - 1, LINE_MOST, block, width), dtype),
            each(SIDE, LINE_MOST, block, width),
            pltpu.VMEM((2, 3, SIDE - 1, PLANE_MOST, block, width), dtype),
            each(SIDE, PLANE_MOST, block, width),
            each(SIDE, LINE_MOST, block, width),
            pltpu.SemaphoreType.DMA((2, 2, 3)),
            pltpu.SemaphoreType.DMA((5, 2, 3)),
            pltpu.SemaphoreType.DMA((5, 2, 3)),
        ],
        compiler_params=pltpu.CompilerParams(
            collective_id=1, has_side_effects=True, vmem_limit_bytes=56 * 1024 * 1024
        ),
        cost_estimate=pl.CostEstimate(flops=0, bytes_accessed=400_000_000, transcendentals=0),
    )(two, three, four, five, expert_in, expert_out)


def relocate_everywhere(expert_in, expert_out, move_slots, myself):
    hidden_units, width = expert_in.shape
    device_count = lax.axis_size("gx") * lax.axis_size("gy")
    sources, targets = move_slots[:, 0], move_slots[:, 1]
    devices = jnp.arange(device_count, dtype=jnp.int32)
    anchor = jnp.sum(jnp.where(targets[None, :] == devices[:, None], sources[None, :], 0), axis=1)
    shape = (device_count, hidden_units // device_count, width)
    results = []
    for weights in (expert_in, expert_out):
        held = lax.all_to_all(weights.reshape(shape), ("gx", "gy"), split_axis=0, concat_axis=0, tiled=True)
        forward = jnp.take(held, anchor, axis=0)
        back = lax.all_to_all(forward, ("gx", "gy"), split_axis=0, concat_axis=0, tiled=True)
        results.append(back.reshape(hidden_units, width))
    return results


def shards(
    tokens_one,
    gates_one,
    routes_one,
    old_place,
    move_slots,
    tokens_two,
    gates_two,
    routes_two,
    expert_in,
    expert_out,
):
    experts_all = old_place.shape[0]
    tokens_here, width = tokens_one.shape
    device_count = lax.axis_size("gx") * lax.axis_size("gy")
    capacity = 2 * tokens_here // device_count
    myself = lax.axis_index(("gx", "gy")).astype(jnp.int32)
    columns = jnp.arange(experts_all, dtype=jnp.int32)
    weights_in, weights_out = expert_in[0], expert_out[0]

    slot_one = jnp.sum(jnp.where(routes_one == columns[None, :], old_place[None, :], 0), axis=1)
    came = jnp.sum(
        jnp.where(routes_two == move_slots[None, :, 1], move_slots[None, :, 0] - routes_two, 0), axis=1
    )
    slot_two = routes_two[:, 0] + came
    layout_one = slot_one * (2 * capacity) + bucket_layout(slot_one, experts_all)
    layout_two = slot_two * (2 * capacity) + capacity + bucket_layout(slot_two, experts_all)
    layout = jnp.concatenate([layout_one, layout_two])
    outbox = (
        jnp.zeros((device_count * 2 * capacity, width), jnp.bfloat16)
        .at[layout]
        .set(jnp.concatenate([tokens_one, tokens_two]))
    )
    framed = outbox.reshape(device_count, 2 * capacity, width)
    received = lax.all_to_all(framed, ("gx", "gy"), split_axis=0, concat_axis=0, tiled=True)
    received = received.reshape(device_count * 2 * capacity, width)
    hidden = jnp.einsum("md,fd->mf", received, weights_in, preferred_element_type=jnp.float32)
    hidden = jnp.maximum(hidden, 0.0).astype(jnp.bfloat16)
    produced = jnp.einsum("mf,fd->md", hidden, weights_out, preferred_element_type=jnp.float32)
    produced = produced.astype(jnp.bfloat16).reshape(framed.shape)
    returned = lax.all_to_all(produced, ("gx", "gy"), split_axis=0, concat_axis=0, tiled=True)
    gathered = returned.reshape(-1, width)[layout].astype(jnp.float32)
    mixed_one = (gates_one[:, None] * gathered[:tokens_here]).astype(jnp.bfloat16)
    mixed_two = (gates_two[:, None] * gathered[tokens_here:]).astype(jnp.bfloat16)

    two, three, four, five, fits = plan_tables(move_slots, myself)
    arrived_in, arrived_out = lax.cond(
        fits,
        lambda: tuple(relocate_lines(weights_in, weights_out, two, three, four, five)),
        lambda: tuple(relocate_everywhere(weights_in, weights_out, move_slots, myself)),
    )
    arriving = jnp.any(move_slots[:, 1] == myself)
    fresh_in = jnp.where(arriving, arrived_in, weights_in)[None]
    fresh_out = jnp.where(arriving, arrived_out, weights_out)[None]
    return (mixed_one, mixed_two, fresh_in, fresh_out)


def solution(mesh):
    return jax.shard_map(
        shards,
        mesh=mesh,
        in_specs=(
            P(("gx", "gy"), None),
            P(("gx", "gy")),
            P(("gx", "gy"), None),
            P(),
            P(),
            P(("gx", "gy"), None),
            P(("gx", "gy")),
            P(("gx", "gy"), None),
            P(("gx", "gy"), None, None),
            P(("gx", "gy"), None, None),
        ),
        out_specs=(
            P(("gx", "gy"), None),
            P(("gx", "gy"), None),
            P(("gx", "gy"), None, None),
            P(("gx", "gy"), None, None),
        ),
        check_vma=False,
    )
```

time: 357 us -> 244 us (0.68)
  Pallas kernels: 0 us -> 146 us
  blocking collectives: 139 us -> 0 us
  waiting for transfers between devices: 123 us -> 40 us
  local copies, waits for them, and re-layouts: 23.6 us -> 3.79 us
  starting transfers between devices: 28.7 us -> 11 us
    pallas_call x0 -> x1, Pallas kernels: none -> 146 us  [relocate_lines(): pl.pallas_call(relocate_kernel, out_shape=[jax.ShapeDtypeStruct((hidden_u...]
    all_to_all x2 -> x0, blocking collectives: 139 us -> none  [the longest x1 70.3 us: relocate(): lax.all_to_all(depart_out.reshape(flat_shape), ('gx', 'gy'), split_axis=0...]
    all_to_all x6 -> x2, waiting for transfers between devices: 123 us -> 40 us  [the longest x1 24.3 us: shards(): lax.all_to_all(framed, ('gx', 'gy'), split_axis=0, concat_axis=0, tiled=T...]
    select_n x6 -> x3, other arithmetic: 19.8 us -> 0.79 us  [the longest x1 0.78 us: coordinates(): device // (LINE * SIDE)]
    all_to_all x6 -> x2, starting transfers between devices: 28.7 us -> 11 us  [the longest x1 6.5 us: shards(): lax.all_to_all(framed, ('gx', 'gy'), split_axis=0, concat_axis=0, tiled=T...]
    gather x4 -> x1, local copies, waits for them, and re-layouts: 13.1 us -> 2.02 us  [shards(): gathered = returned.reshape(-1, width)[layout].astype(jnp.float32)]
    broadcast_in_dim x0 -> x5, other arithmetic: none -> 9.33 us  [the longest x1 5.98 us: shards(): fresh_out = jnp.where(arriving, arrived_out, weights_out)[None]]
    scatter x2 -> x0, local copies, waits for them, and re-layouts: 4.87 us -> none  [run_batch(): outbox = jnp.zeros((local_slots * device_count * capacity, width), jnp.bf...]
  transfers between devices with their start and end apart: 6 -> 2, of which waited for: 5 -> 2; matrix products, arithmetic and copies ran while one was open for 18% -> 4% of each run, Pallas kernels for 0% -> 0%
where the time goes in v1:
time: 244 us; the launch traced here: 243 us
  Pallas kernels  146 us (60%)
  waiting for transfers between devices  40 us (16%)
  other arithmetic  24.5 us (10%)
  matrix products  15 us (6%)
  starting transfers between devices  11 us (5%)
  local copies, waits for them, and re-layouts  3.79 us (2%)
  between operations  2.95 us (1%)
    pallas_call x1, Pallas kernels, relocate_lines(): pl.pallas_call(relocate_kernel, out_shape=[jax.ShapeDtypeStruct((hidden_u...  146 us
    all_to_all x1, waiting for transfers between devices, shards(): lax.all_to_all(framed, ('gx', 'gy'), split_axis=0, concat_axis=0, tiled=T...  24.3 us
    all_to_all x1, waiting for transfers between devices, shards(): lax.all_to_all(produced, ('gx', 'gy'), split_axis=0, concat_axis=0, tiled...  15.7 us
    dot_general x1, matrix products, shards(): jnp.einsum('mf,fd->md', hidden, weights_out, preferred_element_type=jnp.f...  15 us
    all_to_all x1, starting transfers between devices, shards(): lax.all_to_all(framed, ('gx', 'gy'), split_axis=0, concat_axis=0, tiled=T...  6.5 us
    broadcast_in_dim x1, other arithmetic, shards(): fresh_out = jnp.where(arriving, arrived_out, weights_out)[None]  5.98 us
  transfers between devices with their start and end apart: 2, of which 2 were waited for; matrix products, arithmetic and copies ran while one was open for 4% of the time, Pallas kernels for 0%

profile of v1, /device:TPU:1, one launch (start us, length us, event | category | flops | bytes accessed | tf_op | source)
XLA Modules:
  0.0 243.4 jit_solution(6167535322448924582)
XLA Ops:
  0.7 0.8 negate_select_fusion.15
  1.5 0.8 and_select_fusion.6
  2.3 0.8 slice_bitcast_fusion.5
  3.0 0.3 convert_reduce_fusion
  3.4 0.6 reduce_max.27
  4.7 0.6 reduce_max.28
  6.0 0.6 reduce_max.29
  7.3 0.8 select_reduce_fusion.6
  8.0 0.7 add.415
  8.8 0.2 fusion.36
  9.1 0.2 fusion.37
  9.3 0.9 select_reduce_fusion.5
  10.3 0.2 fusion.35
  10.6 0.2 fusion.38
  11.0 149.3 %conditional.1 = ((bf16[3072,768]{1,0:T(8,128)(2,1)}, bf16[3072,768]{1,0:T(8,128)(2,1)})) conditional(s32[]{:T(128)} %convert_element_type.47, (bf16[1,3072,768]{2,1,0:T(8,128)(2,1)}, s32[25,2]{0,1:T(2,128)}, bf16[1,3072,768]{2,1,0:T(8,128)(2,1)}) %tuple.71, (s32[3,1,25]{2,1,0:T(1,128)S(1)}, s32[3,1,25]{2,1,0:T(1,128)S(1)}, s32[3]{0:T(128)S(1)}, ...), branch_computations={%region_16.19_spmd, %region_18.24_spmd} | conditional | flops 4730240 | bytes 400028576 | solution.py:346
  11.2 0.7 select_reduce_fusion.four
  11.9 0.7 select_reduce_fusion.1.three
  12.7 0.7 select_reduce_fusion.2.five
  13.4 0.2 select_reduce_fusion.3
  13.6 0.7 copy.42.two
  14.2 146.1 %branch_1_fun.1 = (bf16[3072,768]{1,0:T(8,128)(2,1)}, bf16[3072,768]{1,0:T(8,128)(2,1)}) custom-call(s32[3,5]{1,0:T(4,128)} %copy.42.two, s32[3,24]{1,0:T(4,128)} %select_reduce_fusion.1.three, s32[3,20]{1,0:T(4,128)} %select_reduce_fusion.four, s32[3,8]{1,0:T(4,128)} %select_reduce_fusion.2.five, bf16[3072,768]{1,0:T(8,128)(2,1)} %get-tuple-element.214.w_in, ...), custom_call_target="tpu_custom_call" | custom-call | bytes 400000000 | tf_op jit(solution)/shard_map/cond/branch_1_fun/pallas_call | solution.py:261
  160.4 3.8 %scatter_custom_fusion = bf16[1024,768]{1,0:T(8,128)(2,1)} fusion(s32[512]{0:T(512)S(1)} %bitcast.230, bf16[256,768]{1,0:T(8,128)(2,1)S(1)} %copy-done, bf16[]{:T(256)} %constant.210, bf16[256,768]{1,0:T(8,128)(2,1)S(1)} %copy-done.1, bf16[]{:T(256)} %constant.178.clone.1), kind=kCustom, calls=%fused_computation.67 | custom fusion | flops 1572864 | bytes 2359300 | tf_op jit(solution)/shard_map/scatter | solution.py:331
  164.2 6.5 %all-to-all-start.4 = ((bf16[128,8,768]{2,1,0:T(8,128)(2,1)}), bf16[128,8,768]{2,1,0:T(8,128)(2,1)S(1)}, u32[]{:S(2)}, u32[]{:S(2)}) async-start(bf16[128,8,768]{2,1,0:T(8,128)(2,1)} %bitcast.40), calls=%async_computation.4 | async-start | bytes 3145728 | tf_op jit(solution)/shard_map/all_to_all | solution.py:334
  170.7 0.6 compare_reduce_fusion
  171.4 24.3 %all-to-all-done.4 = bf16[128,8,768]{2,1,0:T(8,128)(2,1)S(1)} async-done(((bf16[128,8,768]{2,1,0:T(8,128)(2,1)}), bf16[128,8,768]{2,1,0:T(8,128)(2,1)S(1)}, u32[]{:S(2)}, u32[]{:S(2)}) %all-to-all-start.4) | async-done | bytes 1572896 | tf_op jit(solution)/shard_map/all_to_all | solution.py:334
  195.7 15.0 %fusion.25 = bf16[128,8,768]{2,1,0:T(8,128)(2,1)} fusion(bf16[128,8,768]{2,1,0:T(8,128)(2,1)S(1)} %all-to-all-done.4, bf16[1,3072,768]{2,1,0:T(8,128)(2,1)} %param.23, bf16[1,3072,768]{2,1,0:T(8,128)(2,1)} %param.22), kind=kOutput, calls=%fused_computation.62 | convolution fusion | flops 9670754304 | bytes 12582912 | tf_op jit(solution)/shard_map/mf,fd->md/dot_general | solution.py:338
  210.7 4.5 %all-to-all-start.5 = ((bf16[128,8,768]{2,1,0:T(8,128)(2,1)}), bf16[128,8,768]{2,1,0:T(8,128)(2,1)S(1)}, u32[]{:S(2)}, u32[]{:S(2)}) async-start(bf16[128,8,768]{2,1,0:T(8,128)(2,1)} %fusion.25), calls=%async_computation.5 | async-start | bytes 3145728 | tf_op jit(solution)/shard_map/all_to_all | solution.py:340
  215.2 6.0 %select_bitcast_fusion = bf16[1,3072,768]{2,1,0:T(8,128)(2,1)} fusion(bf16[3072,768]{1,0:T(8,128)(2,1)} %get-tuple-element.223, pred[]{:T(512)} %compare_reduce_fusion, bf16[1,3072,768]{2,1,0:T(8,128)(2,1)} %param.23), kind=kLoop, calls=%fused_computation.58 | loop fusion | flops 2359296 | bytes 14155777 | tf_op jit(solution)/shard_map/broadcast_in_dim | solution.py:353
  221.2 3.3 %select_bitcast_fusion.1 = bf16[1,3072,768]{2,1,0:T(8,128)(2,1)} fusion(bf16[3072,768]{1,0:T(8,128)(2,1)} %get-tuple-element.222, pred[]{:T(512)} %compare_reduce_fusion, bf16[1,3072,768]{2,1,0:T(8,128)(2,1)S(1)} %bitcast.216), kind=kLoop, calls=%fused_computation.59 | loop fusion | flops 2359296 | bytes 14155777 | tf_op jit(solution)/shard_map/broadcast_in_dim | solution.py:352
  224.5 15.7 %all-to-all-done.5 = bf16[128,8,768]{2,1,0:T(8,128)(2,1)S(1)} async-done(((bf16[128,8,768]{2,1,0:T(8,128)(2,1)}), bf16[128,8,768]{2,1,0:T(8,128)(2,1)S(1)}, u32[]{:S(2)}, u32[]{:S(2)}) %all-to-all-start.5) | async-done | bytes 1572896 | tf_op jit(solution)/shard_map/all_to_all | solution.py:340
  240.2 2.0 gather_fusion.2
  242.4 1.0 fusion.28
  (51 shorter events, 0.8 us)
Async XLA Ops:
  11.0 149.4 %copy-start = (bf16[256,768]{1,0:T(8,128)(2,1)S(1)}, bf16[256,768]{1,0:T(8,128)(2,1)}, u32[]{:S(2)}) copy-start(bf16[256,768]{1,0:T(8,128)(2,1)} %param.19) | copy-start | bytes 1179652
  11.0 149.4 %copy-start.1 = (bf16[256,768]{1,0:T(8,128)(2,1)S(1)}, bf16[256,768]{1,0:T(8,128)(2,1)}, u32[]{:S(2)}) copy-start(bf16[256,768]{1,0:T(8,128)(2,1)} %param.14) | copy-start | bytes 1179652
  160.4 10.3 %copy-start.2 = (s32[25,2]{0,1:T(2,128)S(1)}, s32[25,2]{0,1:T(2,128)}, u32[]{:S(2)}) copy-start(s32[25,2]{0,1:T(2,128)} %param.18) | copy-start | bytes 604
  164.2 31.4 %all-to-all-start.4 = ((bf16[128,8,768]{2,1,0:T(8,128)(2,1)}), bf16[128,8,768]{2,1,0:T(8,128)(2,1)S(1)}, u32[]{:S(2)}, u32[]{:S(2)}) async-start(bf16[128,8,768]{2,1,0:T(8,128)(2,1)} %bitcast.40), calls=%async_computation.4 | async-start | bytes 3145728 | tf_op jit(solution)/shard_map/all_to_all | solution.py:334
  210.7 10.5 %slice-start = ((s8[4718592]{0:T(1024)(128)(4,1)}), s8[524288]{0:T(1024)(128)(4,1)S(1)}, s32[]{:S(2)}) async-start(s8[4718592]{0:T(1024)(128)(4,1)} %bitcast.215), calls=%async_computation.6 | async-start | bytes 1048576
  210.7 29.5 %all-to-all-start.5 = ((bf16[128,8,768]{2,1,0:T(8,128)(2,1)}), bf16[128,8,768]{2,1,0:T(8,128)(2,1)S(1)}, u32[]{:S(2)}, u32[]{:S(2)}) async-start(bf16[128,8,768]{2,1,0:T(8,128)(2,1)} %fusion.25), calls=%async_computation.5 | async-start | bytes 3145728 | tf_op jit(solution)/shard_map/all_to_all | solution.py:340
  215.2 6.0 %slice-start.1 = ((s8[4718592]{0:T(1024)(128)(4,1)}), s8[4194304]{0:T(1024)(128)(4,1)S(1)}, s32[]{:S(2)}) async-start(s8[4718592]{0:T(1024)(128)(4,1)} %bitcast.215), calls=%async_computation.7 | async-start | bytes 8388608
  240.2 2.1 copy-start.4
  240.2 2.2 copy-start.5

commit v2 on v1

v2 whole, which is shorter than its diff:
```python
import jax
import jax.numpy as jnp
from jax import lax
from jax.experimental import pallas as pl
from jax.experimental.pallas import tpu as pltpu
from jax.sharding import PartitionSpec as P

MESH = pl.DeviceIdType.MESH
SIDE = 4
CORES = 2
LINE = SIDE * CORES
TURNS = ((0, 1, 2), (1, 2, 0), (2, 0, 1))
LINE_MOST = 5
PLANE_MOST = 6
HALVES = 2
BATCHES = 2


def coordinates(device):
    return ((device // CORES) % SIDE, (device // LINE) % SIDE, device // (LINE * SIDE)), device % CORES


def mesh_id(place, core):
    x, y, z = place
    return (z * SIDE + y, x * CORES + core)


def iota(shape, axis):
    return lax.broadcasted_iota(jnp.int32, shape, axis)


def as_row(column):
    count = column.shape[0]
    return jnp.sum(jnp.where(iota((count, count), 0) == iota((count, count), 1), column, 0), axis=0, keepdims=True)


def as_column(row):
    count = row.shape[1]
    return jnp.sum(jnp.where(iota((count, count), 0) == iota((count, count), 1), row, 0), axis=1, keepdims=True)


def rank_in(group):
    count = group.shape[0]
    same = (group == as_row(group)) & (iota((count, count), 1) < iota((count, count), 0))
    return jnp.sum(jnp.where(same, 1, 0), axis=1, keepdims=True)


def split_rows(blocks):
    count, tall, half = blocks.shape
    wide = blocks.astype(jnp.float32)
    left = wide[:, : tall // 2].reshape(count * tall // 2, half)
    right = wide[:, tall // 2 :].reshape(count * tall // 2, half)
    return jnp.concatenate([left, right], axis=1)


def join_rows(rows, tall):
    count, width = rows.shape[0] // (tall // 2), rows.shape[1]
    left = rows[:, : width // 2].reshape(count, tall // 2, width // 2)
    right = rows[:, width // 2 :].reshape(count, tall // 2, width // 2)
    return jnp.concatenate([left, right], axis=1)


def layer_kernel(
    tokens_one, tokens_two, gates_one, gates_two, routes_one, routes_two, old_place, moves, w_in, w_out,
    mixed_one, mixed_two, fits, new_in, new_out,
    first, sent, spread, crossed, landed, outbox, mailbox, returned, held_in, held_out, feed, total, mixing,
    plan, table, local, send, recv, token_send, token_recv, loads,
):
    gx, gy = lax.axis_index("gx"), lax.axis_index("gy")
    at, core = (gy // CORES, gx % SIDE, gx // SIDE), gy % CORES
    devices = outbox.shape[0]
    tall = outbox.shape[1]
    capacity = tall // 2
    myself = gx * LINE + gy
    piece = first[0][0].shape[1]
    block = spread[0][0].shape[2]
    third = piece * LINE
    sources, targets = (w_in, w_out), (new_in, new_out)
    others = [(step, flip) for step in range(SIDE) for flip in range(CORES) if (step, flip) != (0, 0)]

    def beside(axis, step, flip=0):
        place = list(at)
        place[axis] = (place[axis] + step) % SIDE
        return place, (core + flip) % CORES

    def flat_id(device):
        return (device // LINE, device % LINE)

    barrier = pltpu.get_barrier_semaphore()

    def greet(step, carry):
        peer = (myself + step) % devices
        pl.semaphore_signal(barrier, inc=1, device_id=flat_id(peer), device_id_type=MESH)
        return carry

    lax.fori_loop(1, devices, greet, 0)
    pl.semaphore_wait(barrier, devices - 1)

    def ship(src, dst, stage, half, turn, place, which):
        pltpu.make_async_remote_copy(
            src_ref=src,
            dst_ref=dst,
            send_sem=send.at[stage, half, turn],
            recv_sem=recv.at[stage, half, turn],
            device_id=mesh_id(place, which),
            device_id_type=MESH,
        ).start()

    def settle(semaphore, ref):
        pltpu.make_async_copy(ref, ref, semaphore).wait()

    def rows(turn, index):
        return pl.ds(pl.multiple_of(turn * third + index * piece, piece), piece)

    def spot(turn):
        return at[TURNS[turn][0]] * CORES + core

    def own_first(half, turn):
        me = spot(turn)
        return pltpu.make_async_copy(
            sources[half].at[rows(turn, me)], first[half][turn].at[me], local.at[0, half, turn]
        )

    def own_last(half, turn):
        me = spot(turn)
        return pltpu.make_async_copy(
            first[half][turn].at[me], targets[half].at[rows(turn, me)], local.at[1, half, turn]
        )

    def stage_one(half):
        for turn in range(3):
            me = spot(turn)
            for step, flip in others:
                place, which = beside(TURNS[turn][0], step, flip)
                index = place[TURNS[turn][0]] * CORES + which
                ship(
                    sources[half].at[rows(turn, index)], first[half][turn].at[me], 0, half, turn, place, which
                )
            own_first(half, turn).start()

    def stage_two(half):
        for turn in range(3):
            b = TURNS[turn][1]
            own_first(half, turn).wait()
            settle(recv.at[0, half, turn], first[half][turn].at[pl.ds(0, LINE - 1)])
            for step in (1, 2, 3, 0):
                place, which = beside(b, step)
                cut = pl.ds(pl.multiple_of(place[b] * block, block), block)

                def take(k, carry):
                    data = first[half][turn][table[4 * turn, k], cut, :]
                    if step == 0:
                        spread[half][turn][at[b], k] = data
                    else:
                        sent[half, turn, step - 1, k] = data
                    return carry

                lax.fori_loop(0, LINE_MOST, take, 0)
                if step:
                    ship(sent.at[half, turn, step - 1, pl.ds(0, LINE_MOST)], spread[half][turn].at[at[b]], 1, half, turn, place, which)

    def stage_three(half):
        for turn in range(3):
            c = TURNS[turn][2]
            settle(recv.at[1, half, turn], spread[half][turn].at[pl.ds(0, SIDE - 1)])
            settle(send.at[1, half, turn], sent.at[half, turn, :, pl.ds(0, LINE_MOST)])
            for step in (1, 2, 3, 0):
                place, which = beside(c, step)

                def take(k, carry):
                    index = table[4 * turn + 1, place[c] * PLANE_MOST + k]
                    data = spread[half][turn][index // LINE_MOST, index % LINE_MOST]
                    if step == 0:
                        crossed[half][turn][at[c], k] = data
                    else:
                        sent[half, turn, step - 1, k] = data
                    return carry

                lax.fori_loop(0, PLANE_MOST, take, 0)
                if step:
                    ship(sent.at[half, turn, step - 1, pl.ds(0, PLANE_MOST)], crossed[half][turn].at[at[c]], 2, half, turn, place, which)

    def stage_four(half):
        for turn in range(3):
            b = TURNS[turn][1]
            settle(recv.at[2, half, turn], crossed[half][turn].at[pl.ds(0, SIDE - 1)])
            settle(send.at[2, half, turn], sent.at[half, turn, :, pl.ds(0, PLANE_MOST)])
            for step in (1, 2, 3, 0):
                place, which = beside(b, step)

                def take(k, carry):
                    index = table[4 * turn + 2, place[b] * LINE_MOST + k]
                    data = crossed[half][turn][index // PLANE_MOST, index % PLANE_MOST]
                    if step == 0:
                        landed[half][turn][at[b], k] = data
                    else:
                        sent[half, turn, step - 1, k] = data
                    return carry

                lax.fori_loop(0, LINE_MOST, take, 0)
                if step:
                    ship(sent.at[half, turn, step - 1, pl.ds(0, LINE_MOST)], landed[half][turn].at[at[b]], 3, half, turn, place, which)

    def stage_five(half):
        for turn in range(3):
            me = spot(turn)
            settle(recv.at[3, half, turn], landed[half][turn].at[pl.ds(0, SIDE - 1)])
            for step, flip in others + [(0, 0)]:
                place, which = beside(TURNS[turn][0], step, flip)
                index = place[TURNS[turn][0]] * CORES + which
                chosen = table[4 * turn + 3, index]

                def take(quarter, carry):
                    first[half][turn][index, pl.ds(pl.multiple_of(quarter * block, block), block), :] = landed[half][turn][
                        quarter, chosen
                    ]
                    return carry

                lax.fori_loop(0, SIDE, take, 0)
                if (step, flip) != (0, 0):
                    ship(
                        first[half][turn].at[index], targets[half].at[rows(turn, me)], 4, half, turn, place, which
                    )
            own_last(half, turn).start()

    def make_plan():
        source, target = moves[:, 0:1], moves[:, 1:2]
        count = source.shape[0]
        s_at, s_core = coordinates(source)
        t_at, t_core = coordinates(target)
        wide = (count, plan.shape[1])
        entry = iota(wide, 1)
        worst = jnp.zeros((1, 1), jnp.int32)
        plan[...] = jnp.zeros(plan.shape, jnp.int32)
        for turn, (a, b, c) in enumerate(TURNS):
            s_line, t_line = s_at[b] * SIDE + s_at[c], t_at[b] * SIDE + t_at[c]
            rank_s, rank_t, rank_p = rank_in(s_line), rank_in(t_line), rank_in(s_at[c] * SIDE + t_at[c])
            over = jnp.maximum(jnp.maximum(rank_s, rank_t) - LINE_MOST, rank_p - PLANE_MOST) + 1
            worst = jnp.maximum(worst, jnp.max(over, axis=0, keepdims=True))
            rank_s, rank_t = jnp.minimum(rank_s, LINE_MOST - 1), jnp.minimum(rank_t, LINE_MOST - 1)
            rank_p = jnp.minimum(rank_p, PLANE_MOST - 1)
            here = at[b] * SIDE + at[c]
            for row, (mine, slot, value, largest) in enumerate(
                (
                    (s_line == here, rank_s, s_at[a] * CORES + s_core, LINE - 1),
                    (
                        s_at[c] == at[c],
                        t_at[c] * PLANE_MOST + rank_p,
                        s_at[b] * LINE_MOST + rank_s,
                        SIDE * LINE_MOST - 1,
                    ),
                    (
                        t_at[c] == at[c],
                        t_at[b] * LINE_MOST + rank_t,
                        s_at[c] * PLANE_MOST + rank_p,
                        SIDE * PLANE_MOST - 1,
                    ),
                    (t_line == here, t_at[a] * CORES + t_core, rank_t, LINE_MOST - 1),
                )
            ):
                key = jnp.where(mine, slot, -1)
                found = jnp.sum(jnp.where(key == entry, value, 0), axis=0, keepdims=True)
                index = 4 * turn + row
                plan[index : index + 1, :] = jnp.minimum(found, largest)
        fits[...] = jnp.broadcast_to(worst, fits.shape)
        copy = pltpu.make_async_copy(plan, table, loads.at[2])
        copy.start()
        copy.wait()

    def positions():
        routes = routes_one[...]
        slot_one = jnp.sum(
            jnp.where(routes == iota((routes.shape[0], old_place.shape[1]), 1), old_place[...], 0),
            axis=1,
            keepdims=True,
        )
        goal = routes_two[...]
        source, target = as_row(moves[:, 0:1]), as_row(moves[:, 1:2])
        slot_two = goal + jnp.sum(jnp.where(goal == target, source - goal, 0), axis=1, keepdims=True)
        place_one = slot_one * capacity + rank_in(slot_one)
        place_two = slot_two * capacity + capacity // BATCHES + rank_in(slot_two)
        return place_one, place_two

    def one_hot(mask):
        return jnp.where(mask, 1.0, 0.0).astype(jnp.bfloat16)

    def fill_outbox(place_one, place_two):
        row_one, row_two = as_row(place_one), as_row(place_two)
        group = 16
        count = group * capacity

        def fill(index, carry):
            rows_here = iota((count, row_one.shape[1]), 0) + index * count
            picked = jnp.dot(one_hot(rows_here == row_one), tokens_one[...], preferred_element_type=jnp.float32)
            picked += jnp.dot(one_hot(rows_here == row_two), tokens_two[...], preferred_element_type=jnp.float32)
            outbox[pl.ds(index * group, group)] = join_rows(picked, tall).astype(jnp.bfloat16)
            return carry

        lax.fori_loop(0, devices // group, fill, 0)

    def post(src, dst, way, peer):
        pltpu.make_async_remote_copy(
            src_ref=src,
            dst_ref=dst,
            send_sem=token_send.at[way],
            recv_sem=token_recv.at[way],
            device_id=flat_id(peer),
            device_id_type=MESH,
        ).start()

    def send_tokens():
        def go(step, carry):
            peer = (myself + step) % devices
            post(outbox.at[peer], mailbox.at[myself], 0, peer)
            return carry

        lax.fori_loop(1, devices, go, 0)
        mailbox[myself] = outbox[myself]

    group = 32
    tile = 512

    def experts(index):
        begin = index * group
        feed[...] = split_rows(mailbox[pl.ds(begin, group)]).astype(jnp.bfloat16)
        total[...] = jnp.zeros(total.shape, jnp.float32)

        def part(step, carry):
            cut = pl.ds(pl.multiple_of(step * tile, tile), tile)
            hidden = lax.dot_general(
                feed[...], held_in[cut, :], (((1,), (1,)), ((), ())), preferred_element_type=jnp.float32
            )
            hidden = jnp.maximum(hidden, 0.0).astype(jnp.bfloat16)
            total[...] += jnp.dot(hidden, held_out[cut, :], preferred_element_type=jnp.float32)
            return carry

        lax.fori_loop(0, held_in.shape[0] // tile, part, 0)
        mailbox[pl.ds(begin, group)] = join_rows(total[...], tall).astype(jnp.bfloat16)

        def back(peer, carry):
            @pl.when(peer != myself)
            def _():
                post(mailbox.at[peer], returned.at[myself], 1, peer)

            return carry

        lax.fori_loop(begin, begin + group, back, 0)

    def collect(place_one, place_two):
        count = group * capacity
        mixing[...] = jnp.zeros(mixing.shape, jnp.float32)
        tokens_here = place_one.shape[0]

        def add(index, carry):
            results = split_rows(returned[pl.ds(index * group, group)]).astype(jnp.bfloat16)
            columns = iota((tokens_here, count), 1) + index * count
            for batch, place in enumerate((place_one, place_two)):
                mixing[batch] += jnp.dot(one_hot(columns == place), results, preferred_element_type=jnp.float32)
            return carry

        lax.fori_loop(0, devices // group, add, 0)
        mixed_one[...] = (as_column(gates_one[...]) * mixing[0]).astype(jnp.bfloat16)
        mixed_two[...] = (as_column(gates_two[...]) * mixing[1]).astype(jnp.bfloat16)

    load_in = pltpu.make_async_copy(w_in, held_in, loads.at[0])
    load_out = pltpu.make_async_copy(w_out, held_out, loads.at[1])

    stage_one(0)
    place_one, place_two = positions()
    fill_outbox(place_one, place_two)
    send_tokens()
    stage_one(1)
    load_in.start()
    load_out.start()
    make_plan()
    stage_two(0)
    stage_two(1)
    stage_three(0)
    load_in.wait()
    load_out.wait()
    settle(token_recv.at[0], mailbox.at[pl.ds(0, devices - 1)])
    experts(0)
    experts(1)
    stage_three(1)
    experts(2)
    experts(3)
    returned[myself] = mailbox[myself]
    stage_four(0)
    stage_four(1)
    stage_five(0)
    stage_five(1)
    settle(token_recv.at[1], returned.at[pl.ds(0, devices - 1)])
    collect(place_one, place_two)
    settle(token_send.at[0], outbox.at[pl.ds(0, devices - 1)])
    settle(token_send.at[1], mailbox.at[pl.ds(0, devices - 1)])

    for half in range(HALVES):
        for turn in range(3):
            settle(send.at[0, half, turn], first[half][turn].at[pl.ds(0, LINE - 1)])
            settle(send.at[3, half, turn], sent.at[half, turn, :, pl.ds(0, LINE_MOST)])
            settle(send.at[4, half, turn], first[half][turn].at[pl.ds(0, LINE - 1)])
            settle(recv.at[4, half, turn], targets[half].at[pl.ds(0, (LINE - 1) * piece)])
            own_last(half, turn).wait()


def layer(tokens_one, tokens_two, gates_one, gates_two, routes_one, routes_two, old_place, moves, w_in, w_out):
    hidden_units, width = w_in.shape
    tokens_here = tokens_one.shape[0]
    devices = lax.axis_size("gx") * lax.axis_size("gy")
    tall = 2 * BATCHES * (2 * tokens_here // devices)
    piece = hidden_units // (3 * LINE)
    block = piece // SIDE
    dtype = w_in.dtype
    vmem = pl.BlockSpec(memory_space=pltpu.VMEM)
    hbm = pl.BlockSpec(memory_space=pl.ANY)
    most = max(LINE_MOST, PLANE_MOST)

    def each(*shape):
        return [[pltpu.VMEM(shape, dtype)] * 3] * HALVES

    return pl.pallas_call(
        layer_kernel,
        out_shape=[jax.ShapeDtypeStruct((tokens_here, width), dtype)] * 2
        + [jax.ShapeDtypeStruct((8, 128), jnp.int32)]
        + [jax.ShapeDtypeStruct((hidden_units, width), dtype)] * 2,
        in_specs=[vmem] * 8 + [hbm] * 2,
        out_specs=[vmem] * 3 + [hbm] * 2,
        scratch_shapes=[
            each(LINE, piece, width),
            pltpu.VMEM((HALVES, 3, SIDE - 1, most, block, width), dtype),
            each(SIDE, LINE_MOST, block, width),
            each(SIDE, PLANE_MOST, block, width),
            each(SIDE, LINE_MOST, block, width),
            pltpu.VMEM((devices, tall, width // 2), dtype),
            pltpu.VMEM((devices, tall, width // 2), dtype),
            pltpu.VMEM((devices, tall, width // 2), dtype),
            pltpu.VMEM((hidden_units, width), dtype),
            pltpu.VMEM((hidden_units, width), dtype),
            pltpu.VMEM((32 * tall // 2, width), dtype),
            pltpu.VMEM((32 * tall // 2, width), jnp.float32),
            pltpu.VMEM((BATCHES, tokens_here, width), jnp.float32),
            pltpu.VMEM((16, 128), jnp.int32),
            pltpu.SMEM((16, 128), jnp.int32),
            pltpu.SemaphoreType.DMA((2, HALVES, 3)),
            pltpu.SemaphoreType.DMA((5, HALVES, 3)),
            pltpu.SemaphoreType.DMA((5, HALVES, 3)),
            pltpu.SemaphoreType.DMA((2,)),
            pltpu.SemaphoreType.DMA((2,)),
            pltpu.SemaphoreType.DMA((3,)),
        ],
        compiler_params=pltpu.CompilerParams(
            collective_id=1, has_side_effects=True, vmem_limit_bytes=60 * 1024 * 1024
        ),
        cost_estimate=pl.CostEstimate(
            flops=8 * tokens_here * hidden_units * width, bytes_accessed=400_000_000, transcendentals=0
        ),
    )(
        tokens_one,
        tokens_two,
        gates_one.reshape(1, tokens_here),
        gates_two.reshape(1, tokens_here),
        routes_one,
        routes_two,
        old_place.reshape(1, -1),
        moves,
        w_in,
        w_out,
    )


def keep_kernel(arriving, came_in, came_out, own_in, own_out, fresh_in, fresh_out, sems):
    def carry(sources):
        parts = 4
        copies = []
        for half, (source, target) in enumerate(zip(sources, (fresh_in, fresh_out))):
            count = source.shape[0] // parts
            for part in range(parts):
                cut = pl.ds(part * count, count)
                copies.append(pltpu.make_async_copy(source.at[cut], target.at[0, cut], sems.at[half, part]))
        for copy in copies:
            copy.start()
        for copy in copies:
            copy.wait()

    @pl.when(arriving[0] != 0)
    def _():
        carry((came_in, came_out))

    @pl.when(arriving[0] == 0)
    def _():
        carry((own_in.at[0], own_out.at[0]))


def keep(arriving, came_in, came_out, own_in, own_out):
    hbm = pl.BlockSpec(memory_space=pl.ANY)
    return pl.pallas_call(
        keep_kernel,
        out_shape=[jax.ShapeDtypeStruct(own_in.shape, own_in.dtype)] * 2,
        in_specs=[pl.BlockSpec(memory_space=pltpu.SMEM)] + [hbm] * 4,
        out_specs=[hbm] * 2,
        scratch_shapes=[pltpu.SemaphoreType.DMA((HALVES, 4))],
    )(arriving, came_in, came_out, own_in, own_out)


def relocate_everywhere(expert_in, expert_out, move_slots, myself):
    hidden_units, width = expert_in.shape
    device_count = lax.axis_size("gx") * lax.axis_size("gy")
    sources, targets = move_slots[:, 0], move_slots[:, 1]
    devices = jnp.arange(device_count, dtype=jnp.int32)
    anchor = jnp.sum(jnp.where(targets[None, :] == devices[:, None], sources[None, :], 0), axis=1)
    shape = (device_count, hidden_units // device_count, width)
    results = []
    for weights in (expert_in, expert_out):
        held = lax.all_to_all(weights.reshape(shape), ("gx", "gy"), split_axis=0, concat_axis=0, tiled=True)
        forward = jnp.take(held, anchor, axis=0)
        back = lax.all_to_all(forward, ("gx", "gy"), split_axis=0, concat_axis=0, tiled=True)
        results.append(back.reshape(hidden_units, width))
    return results


def shards(
    tokens_one,
    gates_one,
    routes_one,
    old_place,
    move_slots,
    tokens_two,
    gates_two,
    routes_two,
    expert_in,
    expert_out,
):
    myself = lax.axis_index(("gx", "gy")).astype(jnp.int32)
    weights_in, weights_out = expert_in[0], expert_out[0]
    mixed_one, mixed_two, excess, came_in, came_out = layer(
        tokens_one,
        tokens_two,
        gates_one,
        gates_two,
        routes_one,
        routes_two,
        old_place,
        move_slots,
        weights_in,
        weights_out,
    )
    came_in, came_out = lax.cond(
        excess[0, 0] == 0,
        lambda: (came_in, came_out),
        lambda: tuple(relocate_everywhere(weights_in, weights_out, move_slots, myself)),
    )
    arriving = jnp.any(move_slots[:, 1] == myself).astype(jnp.int32).reshape(1)
    fresh_in, fresh_out = keep(arriving, came_in, came_out, expert_in, expert_out)
    return (mixed_one, mixed_two, fresh_in, fresh_out)


def solution(mesh):
    return jax.shard_map(
        shards,
        mesh=mesh,
        in_specs=(
            P(("gx", "gy"), None),
            P(("gx", "gy")),
            P(("gx", "gy"), None),
            P(),
            P(),
            P(("gx", "gy"), None),
            P(("gx", "gy")),
            P(("gx", "gy"), None),
            P(("gx", "gy"), None, None),
            P(("gx", "gy"), None, None),
        ),
        out_specs=(
            P(("gx", "gy"), None),
            P(("gx", "gy"), None),
            P(("gx", "gy"), None, None),
            P(("gx", "gy"), None, None),
        ),
        check_vma=False,
    )
```

time: 244 us -> 491 us (2.01)
  Pallas kernels: 146 us -> 481 us
  waiting for transfers between devices: 40 us -> 0 us
  other arithmetic: 24.5 us -> 0.64 us
  matrix products: 15 us -> 0 us
  starting transfers between devices: 11 us -> 0 us
    pallas_call x1 -> x2, Pallas kernels: 146 us -> 481 us  [the longest x1 287 us: keep(): pl.pallas_call(keep_kernel, out_shape=[jax.ShapeDtypeStruct(own_in.shape,...]
    all_to_all x2 -> x0, waiting for transfers between devices: 40 us -> none  [the longest x1 24.3 us: shards(): lax.all_to_all(framed, ('gx', 'gy'), split_axis=0, concat_axis=0, tiled=T...]
    dot_general x1 -> x0, matrix products: 15 us -> none  [shards(): jnp.einsum('mf,fd->md', hidden, weights_out, preferred_element_type=jnp.f...]
    all_to_all x2 -> x0, starting transfers between devices: 11 us -> none  [the longest x1 6.5 us: shards(): lax.all_to_all(framed, ('gx', 'gy'), split_axis=0, concat_axis=0, tiled=T...]
    broadcast_in_dim x5 -> x0, other arithmetic: 9.33 us -> none  [the longest x1 5.98 us: shards(): fresh_out = jnp.where(arriving, arrived_out, weights_out)[None]]
    unnamed x16 -> x11, local copies, waits for them, and re-layouts: 0.05 us -> 5.82 us
  transfers between devices with their start and end apart: 2 -> 0, of which waited for: 2 -> 0; matrix products, arithmetic and copies ran while one was open for 4% -> 0% of each run, Pallas kernels for 0% -> 0%
where the time goes in v2:
time: 491 us; the launch traced here: 490 us
  Pallas kernels  481 us (98%)
  local copies, waits for them, and re-layouts  7.01 us (1%)
    pallas_call x1, Pallas kernels, keep(): pl.pallas_call(keep_kernel, out_shape=[jax.ShapeDtypeStruct(own_in.shape,...  287 us
    pallas_call x1, Pallas kernels, layer(): pl.pallas_call(layer_kernel, out_shape=[jax.ShapeDtypeStruct((tokens_here...  194 us

profile of v2, /device:TPU:1, one launch (start us, length us, event | category | flops | bytes accessed | tf_op | source)
XLA Modules:
  0.0 490.5 jit_solution(17432872010053659725)
XLA Ops:
  0.6 1.5 copy.17.routes_one
  2.1 1.5 copy.18.routes_two
  3.6 1.4 copy.19.moves
  4.9 0.0 copy-start.2
  4.9 193.7 %shard_map.129 = (bf16[256,768]{1,0:T(8,128)(2,1)}, bf16[256,768]{1,0:T(8,128)(2,1)}, s32[8,128]{1,0:T(8,128)}, bf16[3072,768]{1,0:T(8,128)(2,1)}, bf16[3072,768]{1,0:T(8,128)(2,1)}) custom-call(bf16[256,768]{1,0:T(8,128)(2,1)} %tokens_one.1, bf16[256,768]{1,0:T(8,128)(2,1)} %tokens_two.1, f32[1,256]{1,0:T(1,128)} %bitcast.21, f32[1,256]{1,0:T(1,128)} %bitcast.22, ...), custom_call_target="tpu_custom_call" | custom-call | flops 4831838208 | bytes 400000000 | tf_op jit(solution)/shard_map/pallas_call | solution.py:421
  198.7 1.2 slice.13
  200.5 0.0 copy-done.2
  200.6 0.6 compare_reduce_fusion
  201.8 0.0 copy-start.1
  201.9 0.0 copy-start
  201.9 287.1 %shard_map.130 = (bf16[1,3072,768]{2,1,0:T(8,128)(2,1)}, bf16[1,3072,768]{2,1,0:T(8,128)(2,1)}) custom-call(s32[1]{0:T(128)} %bitcast.11.arriving, bf16[3072,768]{1,0:T(8,128)(2,1)} %get-tuple-element.32.came_in, bf16[3072,768]{1,0:T(8,128)(2,1)} %get-tuple-element.33.came_out, bf16[1,3072,768]{2,1,0:T(8,128)(2,1)} %own_in.1, bf16[1,3072,768]{2,1,0:T(8,128)(2,1)} %own_out.1), custom_call_target="tpu_custom_call" | custom-call | tf_op jit(solution)/shard_map/pallas_call | solution.py:496
  489.0 0.0 copy-done.1
  489.0 0.7 copy.26
  489.7 0.0 copy-done
  489.7 0.7 copy.27
  (1 shorter events, 0.0 us)
Async XLA Ops:
  4.9 195.6 %copy-start.2 = (s32[25,2]{0,1:T(2,128)S(1)}, s32[25,2]{0,1:T(2,128)}, u32[]{:S(2)}) copy-start(s32[25,2]{0,1:T(2,128)} %param.18) | copy-start | bytes 604
  201.8 287.1 %copy-start.1 = (bf16[256,768]{1,0:T(8,128)(2,1)S(1)}, bf16[256,768]{1,0:T(8,128)(2,1)}, u32[]{:S(2)}) copy-start(bf16[256,768]{1,0:T(8,128)(2,1)} %get-tuple-element.48) | copy-start | bytes 1179652
  201.9 287.9 %copy-start = (bf16[256,768]{1,0:T(8,128)(2,1)S(1)}, bf16[256,768]{1,0:T(8,128)(2,1)}, u32[]{:S(2)}) copy-start(bf16[256,768]{1,0:T(8,128)(2,1)} %get-tuple-element.49) | copy-start | bytes 1179652

commit v3 on v2

--- a/solution.py
+++ b/solution.py
@@ -62,7 +62,7 @@
 
 def layer_kernel(
     tokens_one, tokens_two, gates_one, gates_two, routes_one, routes_two, old_place, moves, w_in, w_out,
-    mixed_one, mixed_two, fits, new_in, new_out,
+    mixed_one, mixed_two, flags, new_in, new_out,
     first, sent, spread, crossed, landed, outbox, mailbox, returned, held_in, held_out, feed, total, mixing,
     plan, table, local, send, recv, token_send, token_recv, loads,
 ):
@@ -224,7 +224,7 @@
             own_last(half, turn).start()
 
     def make_plan():
-        source, target = moves[:, 0:1], moves[:, 1:2]
+        source, target = as_column(moves[0:1, :]), as_column(moves[1:2, :])
         count = source.shape[0]
         s_at, s_core = coordinates(source)
         t_at, t_core = coordinates(target)
@@ -262,20 +262,22 @@
                 found = jnp.sum(jnp.where(key == entry, value, 0), axis=0, keepdims=True)
                 index = 4 * turn + row
                 plan[index : index + 1, :] = jnp.minimum(found, largest)
-        fits[...] = jnp.broadcast_to(worst, fits.shape)
+        arriving = jnp.max(jnp.where(target == myself, 1, 0), axis=0, keepdims=True)
+        flags[0:1, :] = jnp.broadcast_to(jnp.maximum(worst, 0), (1, flags.shape[1]))
+        flags[1:2, :] = jnp.broadcast_to(arriving, (1, flags.shape[1]))
         copy = pltpu.make_async_copy(plan, table, loads.at[2])
         copy.start()
         copy.wait()
 
     def positions():
-        routes = routes_one[...]
+        routes = as_column(routes_one[...])
         slot_one = jnp.sum(
             jnp.where(routes == iota((routes.shape[0], old_place.shape[1]), 1), old_place[...], 0),
             axis=1,
             keepdims=True,
         )
-        goal = routes_two[...]
-        source, target = as_row(moves[:, 0:1]), as_row(moves[:, 1:2])
+        goal = as_column(routes_two[...])
+        source, target = moves[0:1, :], moves[1:2, :]
         slot_two = goal + jnp.sum(jnp.where(goal == target, source - goal, 0), axis=1, keepdims=True)
         place_one = slot_one * capacity + rank_in(slot_one)
         place_two = slot_two * capacity + capacity // BATCHES + rank_in(slot_two)
@@ -421,7 +423,7 @@
     return pl.pallas_call(
         layer_kernel,
         out_shape=[jax.ShapeDtypeStruct((tokens_here, width), dtype)] * 2
-        + [jax.ShapeDtypeStruct((8, 128), jnp.int32)]
+        + [jax.ShapeDtypeStruct((2, 128), jnp.int32)]
         + [jax.ShapeDtypeStruct((hidden_units, width), dtype)] * 2,
         in_specs=[vmem] * 8 + [hbm] * 2,
         out_specs=[vmem] * 3 + [hbm] * 2,
@@ -459,47 +461,78 @@
         tokens_two,
         gates_one.reshape(1, tokens_here),
         gates_two.reshape(1, tokens_here),
-        routes_one,
-        routes_two,
+        routes_one.reshape(1, tokens_here),
+        routes_two.reshape(1, tokens_here),
         old_place.reshape(1, -1),
-        moves,
+        moves.T,
         w_in,
         w_out,
     )
 
 
-def keep_kernel(arriving, came_in, came_out, own_in, own_out, fresh_in, fresh_out, sems):
-    def carry(sources):
-        parts = 4
-        copies = []
-        for half, (source, target) in enumerate(zip(sources, (fresh_in, fresh_out))):
-            count = source.shape[0] // parts
-            for part in range(parts):
-                cut = pl.ds(part * count, count)
-                copies.append(pltpu.make_async_copy(source.at[cut], target.at[0, cut], sems.at[half, part]))
-        for copy in copies:
-            copy.start()
-        for copy in copies:
-            copy.wait()
-
-    @pl.when(arriving[0] != 0)
+def keep_kernel(flags, came_in, came_out, mixed_one, mixed_two, own_in, own_out, *rest):
+    *outs, through, mixed, load_sems, store_sems = rest
+    parts = load_sems.shape[1]
+    count = through.shape[2]
+    stores = []
+
+    def load(source, half, part):
+        cut = pl.ds(part * count, count)
+        return pltpu.make_async_copy(source.at[cut], through.at[half, part], load_sems.at[half, part])
+
+    def load_all(sources):
+        for part in range(parts):
+            for half, source in enumerate(sources):
+                load(source, half, part).start()
+
+    @pl.when(flags[1, 0] != 0)
     def _():
-        carry((came_in, came_out))
-
-    @pl.when(arriving[0] == 0)
+        load_all((came_in, came_out))
+
+    @pl.when(flags[1, 0] == 0)
     def _():
-        carry((own_in.at[0], own_out.at[0]))
-
-
-def keep(arriving, came_in, came_out, own_in, own_out):
+        load_all((own_in.at[0], own_out.at[0]))
+
+    mixes = [
+        pltpu.make_async_copy(source, mixed.at[batch], load_sems.at[HALVES, batch])
+        for batch, source in enumerate((mixed_one, mixed_two))
+    ]
+    for copy in mixes:
+        copy.start()
+    for part in range(parts):
+        for half in range(HALVES):
+            load(came_in, half, part).wait()
+            cut = pl.ds(part * count, count)
+            stores.append(
+                pltpu.make_async_copy(through.at[half, part], outs[2 + half].at[0, cut], store_sems.at[half, part])
+            )
+            stores[-1].start()
+    for batch, copy in enumerate(mixes):
+        copy.wait()
+        stores.append(pltpu.make_async_copy(mixed.at[batch], outs[batch], store_sems.at[HALVES, batch]))
+        stores[-1].start()
+    for copy in stores:
+        copy.wait()
+
+
+def keep(flags, came_in, came_out, mixed_one, mixed_two, own_in, own_out):
     hbm = pl.BlockSpec(memory_space=pl.ANY)
+    parts = 6
+    hidden_units, width = came_in.shape
+    like = [jax.ShapeDtypeStruct(x.shape, x.dtype) for x in (mixed_one, mixed_two, own_in, own_out)]
     return pl.pallas_call(
         keep_kernel,
-        out_shape=[jax.ShapeDtypeStruct(own_in.shape, own_in.dtype)] * 2,
-        in_specs=[pl.BlockSpec(memory_space=pltpu.SMEM)] + [hbm] * 4,
-        out_specs=[hbm] * 2,
-        scratch_shapes=[pltpu.SemaphoreType.DMA((HALVES, 4))],
-    )(arriving, came_in, came_out, own_in, own_out)
+        out_shape=like,
+        in_specs=[pl.BlockSpec(memory_space=pltpu.SMEM)] + [hbm] * 6,
+        out_specs=[hbm] * 4,
+        scratch_shapes=[
+            pltpu.VMEM((HALVES, parts, hidden_units // parts, width), came_in.dtype),
+            pltpu.VMEM((BATCHES, *mixed_one.shape), mixed_one.dtype),
+            pltpu.SemaphoreType.DMA((HALVES + 1, parts)),
+            pltpu.SemaphoreType.DMA((HALVES + 1, parts)),
+        ],
+        compiler_params=pltpu.CompilerParams(vmem_limit_bytes=56 * 1024 * 1024),
+    )(flags, came_in, came_out, mixed_one, mixed_two, own_in, own_out)
 
 
 def relocate_everywhere(expert_in, expert_out, move_slots, myself):
@@ -532,7 +565,7 @@
 ):
     myself = lax.axis_index(("gx", "gy")).astype(jnp.int32)
     weights_in, weights_out = expert_in[0], expert_out[0]
-    mixed_one, mixed_two, excess, came_in, came_out = layer(
+    mixed_one, mixed_two, flags, came_in, came_out = layer(
         tokens_one,
         tokens_two,
         gates_one,
@@ -545,13 +578,11 @@
         weights_out,
     )
     came_in, came_out = lax.cond(
-        excess[0, 0] == 0,
+        flags[0, 0] == 0,
         lambda: (came_in, came_out),
         lambda: tuple(relocate_everywhere(weights_in, weights_out, move_slots, myself)),
     )
-    arriving = jnp.any(move_slots[:, 1] == myself).astype(jnp.int32).reshape(1)
-    fresh_in, fresh_out = keep(arriving, came_in, came_out, expert_in, expert_out)
-    return (mixed_one, mixed_two, fresh_in, fresh_out)
+    return tuple(keep(flags, came_in, came_out, mixed_one, mixed_two, expert_in, expert_out))
 
 
 def solution(mesh):

time: 491 us -> 205 us (0.42)
  Pallas kernels: 481 us -> 202 us
  local copies, waits for them, and re-layouts: 7.01 us -> 1.2 us
    pallas_call x1, Pallas kernels: 287 us -> 8.66 us  [keep(): pl.pallas_call(keep_kernel, out_shape=like, in_specs=[pl.BlockSpec(memory...]
    unnamed x11 -> x2, local copies, waits for them, and re-layouts: 5.82 us -> 0.01 us
where the time goes in v3:
time: 205 us
  Pallas kernels  202 us (99%)
    pallas_call x1, Pallas kernels, layer(): pl.pallas_call(layer_kernel, out_shape=[jax.ShapeDtypeStruct((tokens_here...  193 us
    pallas_call x1, Pallas kernels, keep(): pl.pallas_call(keep_kernel, out_shape=like, in_specs=[pl.BlockSpec(memory...  8.66 us

profile of v3, /device:TPU:1, one launch (start us, length us, event | category | flops | bytes accessed | tf_op | source)
XLA Modules:
  0.0 204.5 jit_solution(6321606090266975433)
XLA Ops:
  0.6 0.0 copy-start
  0.6 193.3 %shard_map.129 = (bf16[256,768]{1,0:T(8,128)(2,1)}, bf16[256,768]{1,0:T(8,128)(2,1)}, s32[2,128]{1,0:T(2,128)}, bf16[3072,768]{1,0:T(8,128)(2,1)}, bf16[3072,768]{1,0:T(8,128)(2,1)}) custom-call(bf16[256,768]{1,0:T(8,128)(2,1)} %tokens_one.1, bf16[256,768]{1,0:T(8,128)(2,1)} %tokens_two.1, f32[1,256]{1,0:T(1,128)} %bitcast.24, f32[1,256]{1,0:T(1,128)} %bitcast.25, ...), custom_call_target="tpu_custom_call" | custom-call | flops 4831838208 | bytes 400000000 | tf_op jit(solution)/shard_map/pallas_call | solution.py:423
  194.0 1.2 slice.9
  195.8 0.0 copy-done
  195.9 8.7 %shard_map.130 = (bf16[256,768]{1,0:T(8,128)(2,1)}, bf16[256,768]{1,0:T(8,128)(2,1)}, bf16[1,3072,768]{2,1,0:T(8,128)(2,1)}, bf16[1,3072,768]{2,1,0:T(8,128)(2,1)}) custom-call(s32[2,128]{1,0:T(2,128)} %get-tuple-element.25.flags, bf16[3072,768]{1,0:T(8,128)(2,1)} %get-tuple-element.28.came_in, bf16[3072,768]{1,0:T(8,128)(2,1)} %get-tuple-element.29.came_out, ...), custom_call_target="tpu_custom_call" | custom-call | tf_op jit(solution)/shard_map/pallas_call | solution.py:523
  (1 shorter events, 0.0 us)
Async XLA Ops:
  0.6 195.2 %copy-start = (s32[25,2]{0,1:T(2,128)S(1)}, s32[25,2]{0,1:T(2,128)}, u32[]{:S(2)}) copy-start(s32[25,2]{0,1:T(2,128)} %param.18) | copy-start | bytes 604

commit v4 on v3

--- a/solution.py
+++ b/solution.py
@@ -1,3 +1,5 @@
+import functools
+
 import jax
 import jax.numpy as jnp
 from jax import lax
@@ -10,8 +12,7 @@
 CORES = 2
 LINE = SIDE * CORES
 TURNS = ((0, 1, 2), (1, 2, 0), (2, 0, 1))
-LINE_MOST = 5
-PLANE_MOST = 6
+LIMITS = ((4, 4, 8), (5, 5, 8), (6, 6, 8))
 HALVES = 2
 BATCHES = 2
 
@@ -61,13 +62,15 @@
 
 
 def layer_kernel(
+    limits,
     tokens_one, tokens_two, gates_one, gates_two, routes_one, routes_two, old_place, moves, w_in, w_out,
     mixed_one, mixed_two, flags, new_in, new_out,
     first, sent, spread, crossed, landed, outbox, mailbox, returned, held_in, held_out, feed, total, mixing,
-    plan, table, local, send, recv, token_send, token_recv, loads,
+    plan, table, local, send, recv, token_send, token_recv, loads, hello,
 ):
     gx, gy = lax.axis_index("gx"), lax.axis_index("gy")
     at, core = (gy // CORES, gx % SIDE, gx // SIDE), gy % CORES
+    line_most, plane_most, own_most = limits
     devices = outbox.shape[0]
     tall = outbox.shape[1]
     capacity = tall // 2
@@ -87,14 +90,19 @@
         return (device // LINE, device % LINE)
 
     barrier = pltpu.get_barrier_semaphore()
-
-    def greet(step, carry):
-        peer = (myself + step) % devices
-        pl.semaphore_signal(barrier, inc=1, device_id=flat_id(peer), device_id_type=MESH)
-        return carry
-
-    lax.fori_loop(1, devices, greet, 0)
-    pl.semaphore_wait(barrier, devices - 1)
+    peers = [beside(0, 0, 1)] + [
+        beside(axis, step, flip) for axis in range(3) for step in range(1, SIDE) for flip in range(CORES)
+    ]
+    for place, which in peers:
+        pl.semaphore_signal(barrier, inc=1, device_id=mesh_id(place, which), device_id_type=MESH)
+    pl.semaphore_wait(barrier, len(peers))
+
+    def meet_all():
+        for axis in (1, 2):
+            for step in range(1, SIDE):
+                place, which = beside(axis, step)
+                pl.semaphore_signal(hello.at[axis - 1], inc=1, device_id=mesh_id(place, which), device_id_type=MESH)
+            pl.semaphore_wait(hello.at[axis - 1], SIDE - 1)
 
     def ship(src, dst, stage, half, turn, place, which):
         pltpu.make_async_remote_copy(
@@ -155,51 +163,51 @@
                         sent[half, turn, step - 1, k] = data
                     return carry
 
-                lax.fori_loop(0, LINE_MOST, take, 0)
+                lax.fori_loop(0, line_most, take, 0)
                 if step:
-                    ship(sent.at[half, turn, step - 1, pl.ds(0, LINE_MOST)], spread[half][turn].at[at[b]], 1, half, turn, place, which)
+                    ship(sent.at[half, turn, step - 1, pl.ds(0, line_most)], spread[half][turn].at[at[b]], 1, half, turn, place, which)
 
     def stage_three(half):
         for turn in range(3):
             c = TURNS[turn][2]
             settle(recv.at[1, half, turn], spread[half][turn].at[pl.ds(0, SIDE - 1)])
-            settle(send.at[1, half, turn], sent.at[half, turn, :, pl.ds(0, LINE_MOST)])
+            settle(send.at[1, half, turn], sent.at[half, turn, :, pl.ds(0, line_most)])
             for step in (1, 2, 3, 0):
                 place, which = beside(c, step)
 
                 def take(k, carry):
-                    index = table[4 * turn + 1, place[c] * PLANE_MOST + k]
-                    data = spread[half][turn][index // LINE_MOST, index % LINE_MOST]
+                    index = table[4 * turn + 1, place[c] * own_most + k]
+                    data = spread[half][turn][index // line_most, index % line_most]
                     if step == 0:
                         crossed[half][turn][at[c], k] = data
                     else:
                         sent[half, turn, step - 1, k] = data
                     return carry
 
-                lax.fori_loop(0, PLANE_MOST, take, 0)
+                lax.fori_loop(0, plane_most if step else own_most, take, 0)
                 if step:
-                    ship(sent.at[half, turn, step - 1, pl.ds(0, PLANE_MOST)], crossed[half][turn].at[at[c]], 2, half, turn, place, which)
+                    ship(sent.at[half, turn, step - 1, pl.ds(0, plane_most)], crossed[half][turn].at[at[c], pl.ds(0, plane_most)], 2, half, turn, place, which)
 
     def stage_four(half):
         for turn in range(3):
             b = TURNS[turn][1]
-            settle(recv.at[2, half, turn], crossed[half][turn].at[pl.ds(0, SIDE - 1)])
-            settle(send.at[2, half, turn], sent.at[half, turn, :, pl.ds(0, PLANE_MOST)])
+            settle(recv.at[2, half, turn], crossed[half][turn].at[pl.ds(0, SIDE - 1), pl.ds(0, plane_most)])
+            settle(send.at[2, half, turn], sent.at[half, turn, :, pl.ds(0, plane_most)])
             for step in (1, 2, 3, 0):
                 place, which = beside(b, step)
 
                 def take(k, carry):
-                    index = table[4 * turn + 2, place[b] * LINE_MOST + k]
-                    data = crossed[half][turn][index // PLANE_MOST, index % PLANE_MOST]
+                    index = table[4 * turn + 2, place[b] * line_most + k]
+                    data = crossed[half][turn][index // own_most, index % own_most]
                     if step == 0:
                         landed[half][turn][at[b], k] = data
                     else:
                         sent[half, turn, step - 1, k] = data
                     return carry
 
-                lax.fori_loop(0, LINE_MOST, take, 0)
+                lax.fori_loop(0, line_most, take, 0)
                 if step:
-                    ship(sent.at[half, turn, step - 1, pl.ds(0, LINE_MOST)], landed[half][turn].at[at[b]], 3, half, turn, place, which)
+                    ship(sent.at[half, turn, step - 1, pl.ds(0, line_most)], landed[half][turn].at[at[b]], 3, half, turn, place, which)
 
     def stage_five(half):
         for turn in range(3):
@@ -230,32 +238,29 @@
         t_at, t_core = coordinates(target)
         wide = (count, plan.shape[1])
         entry = iota(wide, 1)
-        worst = jnp.zeros((1, 1), jnp.int32)
         plan[...] = jnp.zeros(plan.shape, jnp.int32)
         for turn, (a, b, c) in enumerate(TURNS):
             s_line, t_line = s_at[b] * SIDE + s_at[c], t_at[b] * SIDE + t_at[c]
             rank_s, rank_t, rank_p = rank_in(s_line), rank_in(t_line), rank_in(s_at[c] * SIDE + t_at[c])
-            over = jnp.maximum(jnp.maximum(rank_s, rank_t) - LINE_MOST, rank_p - PLANE_MOST) + 1
-            worst = jnp.maximum(worst, jnp.max(over, axis=0, keepdims=True))
-            rank_s, rank_t = jnp.minimum(rank_s, LINE_MOST - 1), jnp.minimum(rank_t, LINE_MOST - 1)
-            rank_p = jnp.minimum(rank_p, PLANE_MOST - 1)
+            rank_s, rank_t = jnp.minimum(rank_s, line_most - 1), jnp.minimum(rank_t, line_most - 1)
+            rank_p = jnp.minimum(rank_p, own_most - 1)
             here = at[b] * SIDE + at[c]
             for row, (mine, slot, value, largest) in enumerate(
                 (
                     (s_line == here, rank_s, s_at[a] * CORES + s_core, LINE - 1),
                     (
                         s_at[c] == at[c],
-                        t_at[c] * PLANE_MOST + rank_p,
-                        s_at[b] * LINE_MOST + rank_s,
-                        SIDE * LINE_MOST - 1,
+                        t_at[c] * own_most + rank_p,
+                        s_at[b] * line_most + rank_s,
+                        SIDE * line_most - 1,
                     ),
                     (
                         t_at[c] == at[c],
-                        t_at[b] * LINE_MOST + rank_t,
-                        s_at[c] * PLANE_MOST + rank_p,
-                        SIDE * PLANE_MOST - 1,
+                        t_at[b] * line_most + rank_t,
+                        s_at[c] * own_most + rank_p,
+                        SIDE * own_most - 1,
                     ),
-                    (t_line == here, t_at[a] * CORES + t_core, rank_t, LINE_MOST - 1),
+                    (t_line == here, t_at[a] * CORES + t_core, rank_t, line_most - 1),
                 )
             ):
                 key = jnp.where(mine, slot, -1)
@@ -263,8 +268,7 @@
                 index = 4 * turn + row
                 plan[index : index + 1, :] = jnp.minimum(found, largest)
         arriving = jnp.max(jnp.where(target == myself, 1, 0), axis=0, keepdims=True)
-        flags[0:1, :] = jnp.broadcast_to(jnp.maximum(worst, 0), (1, flags.shape[1]))
-        flags[1:2, :] = jnp.broadcast_to(arriving, (1, flags.shape[1]))
+        flags[...] = jnp.broadcast_to(arriving, flags.shape)
         copy = pltpu.make_async_copy(plan, table, loads.at[2])
         copy.start()
         copy.wait()
@@ -368,6 +372,7 @@
     load_out = pltpu.make_async_copy(w_out, held_out, loads.at[1])
 
     stage_one(0)
+    meet_all()
     place_one, place_two = positions()
     fill_outbox(place_one, place_two)
     send_tokens()
@@ -399,13 +404,14 @@
     for half in range(HALVES):
         for turn in range(3):
             settle(send.at[0, half, turn], first[half][turn].at[pl.ds(0, LINE - 1)])
-            settle(send.at[3, half, turn], sent.at[half, turn, :, pl.ds(0, LINE_MOST)])
+            settle(send.at[3, half, turn], sent.at[half, turn, :, pl.ds(0, line_most)])
             settle(send.at[4, half, turn], first[half][turn].at[pl.ds(0, LINE - 1)])
             settle(recv.at[4, half, turn], targets[half].at[pl.ds(0, (LINE - 1) * piece)])
             own_last(half, turn).wait()
 
 
-def layer(tokens_one, tokens_two, gates_one, gates_two, routes_one, routes_two, old_place, moves, w_in, w_out):
+def layer(which, tokens_one, tokens_two, gates_one, gates_two, routes_one, routes_two, old_place, moves, w_in, w_out):
+    line_most, plane_most, own_most = LIMITS[which]
     hidden_units, width = w_in.shape
     tokens_here = tokens_one.shape[0]
     devices = lax.axis_size("gx") * lax.axis_size("gy")
@@ -415,24 +421,24 @@
     dtype = w_in.dtype
     vmem = pl.BlockSpec(memory_space=pltpu.VMEM)
     hbm = pl.BlockSpec(memory_space=pl.ANY)
-    most = max(LINE_MOST, PLANE_MOST)
+    most = max(line_most, plane_most)
 
     def each(*shape):
         return [[pltpu.VMEM(shape, dtype)] * 3] * HALVES
 
     return pl.pallas_call(
-        layer_kernel,
+        functools.partial(layer_kernel, LIMITS[which]),
         out_shape=[jax.ShapeDtypeStruct((tokens_here, width), dtype)] * 2
-        + [jax.ShapeDtypeStruct((2, 128), jnp.int32)]
+        + [jax.ShapeDtypeStruct((1, 128), jnp.int32)]
         + [jax.ShapeDtypeStruct((hidden_units, width), dtype)] * 2,
         in_specs=[vmem] * 8 + [hbm] * 2,
         out_specs=[vmem] * 3 + [hbm] * 2,
         scratch_shapes=[
             each(LINE, piece, width),
             pltpu.VMEM((HALVES, 3, SIDE - 1, most, block, width), dtype),
-            each(SIDE, LINE_MOST, block, width),
-            each(SIDE, PLANE_MOST, block, width),
-            each(SIDE, LINE_MOST, block, width),
+            each(SIDE, line_most, block, width),
+            each(SIDE, own_most, block, width),
+            each(SIDE, line_most, block, width),
             pltpu.VMEM((devices, tall, width // 2), dtype),
             pltpu.VMEM((devices, tall, width // 2), dtype),
             pltpu.VMEM((devices, tall, width // 2), dtype),
@@ -449,9 +455,10 @@
             pltpu.SemaphoreType.DMA((2,)),
             pltpu.SemaphoreType.DMA((2,)),
             pltpu.SemaphoreType.DMA((3,)),
+            pltpu.SemaphoreType.REGULAR((2,)),
         ],
         compiler_params=pltpu.CompilerParams(
-            collective_id=1, has_side_effects=True, vmem_limit_bytes=60 * 1024 * 1024
+            collective_id=1 + which, has_side_effects=True, vmem_limit_bytes=60 * 1024 * 1024
         ),
         cost_estimate=pl.CostEstimate(
             flops=8 * tokens_here * hidden_units * width, bytes_accessed=400_000_000, transcendentals=0
@@ -485,11 +492,11 @@
             for half, source in enumerate(sources):
                 load(source, half, part).start()
 
-    @pl.when(flags[1, 0] != 0)
+    @pl.when(flags[0, 0] != 0)
     def _():
         load_all((came_in, came_out))
 
-    @pl.when(flags[1, 0] == 0)
+    @pl.when(flags[0, 0] == 0)
     def _():
         load_all((own_in.at[0], own_out.at[0]))
 
@@ -535,6 +542,30 @@
     )(flags, came_in, came_out, mixed_one, mixed_two, own_in, own_out)
 
 
+def limits_needed(move_slots):
+    (sx, sy, sz), _ = coordinates(move_slots[:, 0])
+    (tx, ty, tz), _ = coordinates(move_slots[:, 1])
+
+    def same(value):
+        return value[:, None] == value[None, :]
+
+    def counts(*masks):
+        fields = sum(jnp.where(mask, 1 << (5 * i), 0) for i, mask in enumerate(masks))
+        total = jnp.sum(fields, axis=1, dtype=jnp.int32)
+        return [(total >> (5 * i)) & 31 for i in range(len(masks))]
+
+    ex, ey, ez, fx, fy, fz = (same(value) for value in (sx, sy, sz, tx, ty, tz))
+    lines = counts(ey & ez, ez & ex, ex & ey, fy & fz, fz & fx, fx & fy)
+    planes = counts(ez & fz, ex & fx, ey & fy)
+    level = 0
+    for line_most, plane_most, own_most in LIMITS:
+        over = functools.reduce(jnp.logical_or, [count > line_most for count in lines])
+        for count, start, end in zip(planes, (sz, sx, sy), (tz, tx, ty)):
+            over |= count > jnp.where(start == end, own_most, plane_most)
+        level += over.astype(jnp.int32)
+    return jnp.max(level)
+
+
 def relocate_everywhere(expert_in, expert_out, move_slots, myself):
     hidden_units, width = expert_in.shape
     device_count = lax.axis_size("gx") * lax.axis_size("gy")
@@ -565,7 +596,7 @@
 ):
     myself = lax.axis_index(("gx", "gy")).astype(jnp.int32)
     weights_in, weights_out = expert_in[0], expert_out[0]
-    mixed_one, mixed_two, flags, came_in, came_out = layer(
+    operands = (
         tokens_one,
         tokens_two,
         gates_one,
@@ -577,10 +608,14 @@
         weights_in,
         weights_out,
     )
-    came_in, came_out = lax.cond(
-        flags[0, 0] == 0,
-        lambda: (came_in, came_out),
-        lambda: tuple(relocate_everywhere(weights_in, weights_out, move_slots, myself)),
+
+    def beyond():
+        mixed_one, mixed_two, flags, *_ = layer(0, *operands)
+        return (mixed_one, mixed_two, flags, *relocate_everywhere(weights_in, weights_out, move_slots, myself))
+
+    mixed_one, mixed_two, flags, came_in, came_out = lax.switch(
+        limits_needed(move_slots),
+        [lambda which=which: tuple(layer(which, *operands)) for which in range(len(LIMITS))] + [beyond],
     )
     return tuple(keep(flags, came_in, came_out, mixed_one, mixed_two, expert_in, expert_out))
 

time: 205 us -> 187 us (0.912)
  Pallas kernels: 202 us -> 181 us
  other arithmetic: 0 us -> 2.42 us
    pallas_call x1, Pallas kernels: 193 us -> 173 us  [layer(): pl.pallas_call(functools.partial(layer_kernel, LIMITS[which]), out_shape=...]
where the time goes in v4:
time: 187 us; the launch traced here: 186 us
  Pallas kernels  181 us (97%)
  other arithmetic  2.42 us (1%)
    pallas_call x1, Pallas kernels, layer(): pl.pallas_call(functools.partial(layer_kernel, LIMITS[which]), out_shape=...  173 us
    pallas_call x1, Pallas kernels, keep(): pl.pallas_call(keep_kernel, out_shape=like, in_specs=[pl.BlockSpec(memory...  8.15 us

profile of v4, /device:TPU:1, one launch (start us, length us, event | category | flops | bytes accessed | tf_op | source)
XLA Modules:
  0.0 186.2 jit_solution(9588666892909415076)
XLA Ops:
  0.6 0.8 and_select_fusion.4
  1.4 0.8 fusion
  2.2 0.2 add_reduce_fusion
  2.4 0.7 add_reduce_fusion.2
  3.7 174.1 %conditional.1 = ((bf16[256,768]{1,0:T(8,128)(2,1)S(1)}, bf16[256,768]{1,0:T(8,128)(2,1)S(1)}, s32[1,128]{1,0:T(1,128)S(1)}, bf16[3072,768]{1,0:T(8,128)(2,1)}, bf16[3072,768]{1,0:T(8,128)(2,1)})) conditional(s32[]{:T(128)} %clamp.3, (f32[256]{0:T(256)}, f32[256]{0:T(256)}, s32[256,1]{0,1:T(1,128)}, ...), branch_computations={%region_3.4_spmd, %region_4.5_spmd, %region_5.6_spmd, %region_6.9_... | conditional | flops 4836568064 | bytes 488108480 | solution.py:616
  3.7 173.3 %branch_0_fun.1 = (bf16[256,768]{1,0:T(8,128)(2,1)S(1)}, bf16[256,768]{1,0:T(8,128)(2,1)S(1)}, s32[1,128]{1,0:T(1,128)S(1)}, bf16[3072,768]{1,0:T(8,128)(2,1)}, bf16[3072,768]{1,0:T(8,128)(2,1)}) custom-call(bf16[256,768]{1,0:T(8,128)(2,1)} %get-tuple-element.71.tokens_one, bf16[256,768]{1,0:T(8,128)(2,1)} %get-tuple-element.86.tokens_two, ...), custom_call_target="tpu_custom_call" | custom-call | flops 4831838208 | bytes 400000000 | tf_op jit(solution)/shard_map/cond/branch_0_fun/pallas_call | solution.py:429
  177.8 8.1 %shard_map.129 = (bf16[256,768]{1,0:T(8,128)(2,1)}, bf16[256,768]{1,0:T(8,128)(2,1)}, bf16[1,3072,768]{2,1,0:T(8,128)(2,1)}, bf16[1,3072,768]{2,1,0:T(8,128)(2,1)}) custom-call(s32[1,128]{1,0:T(1,128)S(1)} %get-tuple-element.139.flags, bf16[3072,768]{1,0:T(8,128)(2,1)} %get-tuple-element.140.came_in, bf16[3072,768]{1,0:T(8,128)(2,1)} %get-tuple-element.141.came_out, ...), custom_call_target="tpu_custom_call" | custom-call | tf_op jit(solution)/shard_map/pallas_call | solution.py:530

commit v5 on v4

--- a/solution.py
+++ b/solution.py
@@ -316,18 +316,21 @@
 
     def send_tokens():
         def go(step, carry):
-            peer = (myself + step) % devices
-            post(outbox.at[peer], mailbox.at[myself], 0, peer)
+            peer = (myself + step * 79) % devices
+            post(outbox.at[peer], mailbox.at[my_slot], 0, peer)
             return carry
 
         lax.fori_loop(1, devices, go, 0)
-        mailbox[myself] = outbox[myself]
-
-    group = 32
+        mailbox[my_slot] = outbox[myself]
+
+    group = SIDE * LINE
     tile = 512
+    my_sum = (at[0] + at[1] + at[2]) % SIDE
+    my_slot = my_sum * group + myself % group
 
     def experts(index):
-        begin = index * group
+        quarter = (index + my_sum) % SIDE
+        begin = quarter * group
         feed[...] = split_rows(mailbox[pl.ds(begin, group)]).astype(jnp.bfloat16)
         total[...] = jnp.zeros(total.shape, jnp.float32)
 
@@ -343,14 +346,18 @@
         lax.fori_loop(0, held_in.shape[0] // tile, part, 0)
         mailbox[pl.ds(begin, group)] = join_rows(total[...], tall).astype(jnp.bfloat16)
 
-        def back(peer, carry):
+        def back(step, carry):
+            low = (myself + step * 13) % group
+            z = (quarter + 2 * SIDE - (low // LINE) % SIDE - (low // CORES) % SIDE) % SIDE
+            peer = z * group + low
+
             @pl.when(peer != myself)
             def _():
-                post(mailbox.at[peer], returned.at[myself], 1, peer)
+                post(mailbox.at[begin + low], returned.at[myself], 1, peer)
 
             return carry
 
-        lax.fori_loop(begin, begin + group, back, 0)
+        lax.fori_loop(0, group, back, 0)
 
     def collect(place_one, place_two):
         count = group * capacity
@@ -391,7 +398,7 @@
     stage_three(1)
     experts(2)
     experts(3)
-    returned[myself] = mailbox[myself]
+    returned[myself] = mailbox[my_slot]
     stage_four(0)
     stage_four(1)
     stage_five(0)

time: 187 us -> 189 us (1.011)
  Pallas kernels: 181 us -> 184 us
    pallas_call x1, Pallas kernels: 173 us -> 176 us  [layer(): pl.pallas_call(functools.partial(layer_kernel, LIMITS[which]), out_shape=...]
where the time goes in v5:
time: 189 us
  Pallas kernels  184 us (97%)
  other arithmetic  2.42 us (1%)
    pallas_call x1, Pallas kernels, layer(): pl.pallas_call(functools.partial(layer_kernel, LIMITS[which]), out_shape=...  176 us
    pallas_call x1, Pallas kernels, keep(): pl.pallas_call(keep_kernel, out_shape=like, in_specs=[pl.BlockSpec(memory...  8.16 us

profile of v5, /device:TPU:1, one launch (start us, length us, event | category | flops | bytes accessed | tf_op | source)
XLA Modules:
  0.0 188.8 jit_solution(14733069723243437144)
XLA Ops:
  0.6 0.8 and_select_fusion.4
  1.4 0.8 fusion
  2.2 0.2 add_reduce_fusion
  2.4 0.7 add_reduce_fusion.2
  3.7 176.7 %conditional.1 = ((bf16[256,768]{1,0:T(8,128)(2,1)S(1)}, bf16[256,768]{1,0:T(8,128)(2,1)S(1)}, s32[1,128]{1,0:T(1,128)S(1)}, bf16[3072,768]{1,0:T(8,128)(2,1)}, bf16[3072,768]{1,0:T(8,128)(2,1)})) conditional(s32[]{:T(128)} %clamp.3, (f32[256]{0:T(256)}, f32[256]{0:T(256)}, s32[256,1]{0,1:T(1,128)}, ...), branch_computations={%region_3.4_spmd, %region_4.5_spmd, %region_5.6_spmd, %region_6.9_... | conditional | flops 4836568064 | bytes 488108480 | solution.py:623
  3.9 176.0 %branch_1_fun.1 = (bf16[256,768]{1,0:T(8,128)(2,1)S(1)}, bf16[256,768]{1,0:T(8,128)(2,1)S(1)}, s32[1,128]{1,0:T(1,128)S(1)}, bf16[3072,768]{1,0:T(8,128)(2,1)}, bf16[3072,768]{1,0:T(8,128)(2,1)}) custom-call(bf16[256,768]{1,0:T(8,128)(2,1)} %get-tuple-element.95.tokens_one, bf16[256,768]{1,0:T(8,128)(2,1)} %get-tuple-element.96.tokens_two, ...), custom_call_target="tpu_custom_call" | custom-call | flops 4831838208 | bytes 400000000 | tf_op jit(solution)/shard_map/cond/branch_1_fun/pallas_call | solution.py:436
  180.5 8.2 %shard_map.129 = (bf16[256,768]{1,0:T(8,128)(2,1)}, bf16[256,768]{1,0:T(8,128)(2,1)}, bf16[1,3072,768]{2,1,0:T(8,128)(2,1)}, bf16[1,3072,768]{2,1,0:T(8,128)(2,1)}) custom-call(s32[1,128]{1,0:T(1,128)S(1)} %get-tuple-element.139.flags, bf16[3072,768]{1,0:T(8,128)(2,1)} %get-tuple-element.140.came_in, bf16[3072,768]{1,0:T(8,128)(2,1)} %get-tuple-element.141.came_out, ...), custom_call_target="tpu_custom_call" | custom-call | tf_op jit(solution)/shard_map/pallas_call | solution.py:537

commit v6 on v5

--- a/solution.py
+++ b/solution.py
@@ -66,7 +66,7 @@
     tokens_one, tokens_two, gates_one, gates_two, routes_one, routes_two, old_place, moves, w_in, w_out,
     mixed_one, mixed_two, flags, new_in, new_out,
     first, sent, spread, crossed, landed, outbox, mailbox, returned, held_in, held_out, feed, total, mixing,
-    plan, table, local, send, recv, token_send, token_recv, loads, hello,
+    plan, table, local, send, recv, token_send, token_recv, loads, hello, held_tokens,
 ):
     gx, gy = lax.axis_index("gx"), lax.axis_index("gy")
     at, core = (gy // CORES, gx % SIDE, gx // SIDE), gy % CORES
@@ -297,8 +297,8 @@
 
         def fill(index, carry):
             rows_here = iota((count, row_one.shape[1]), 0) + index * count
-            picked = jnp.dot(one_hot(rows_here == row_one), tokens_one[...], preferred_element_type=jnp.float32)
-            picked += jnp.dot(one_hot(rows_here == row_two), tokens_two[...], preferred_element_type=jnp.float32)
+            picked = jnp.dot(one_hot(rows_here == row_one), held_tokens[0], preferred_element_type=jnp.float32)
+            picked += jnp.dot(one_hot(rows_here == row_two), held_tokens[1], preferred_element_type=jnp.float32)
             outbox[pl.ds(index * group, group)] = join_rows(picked, tall).astype(jnp.bfloat16)
             return carry
 
@@ -375,12 +375,20 @@
         mixed_one[...] = (as_column(gates_one[...]) * mixing[0]).astype(jnp.bfloat16)
         mixed_two[...] = (as_column(gates_two[...]) * mixing[1]).astype(jnp.bfloat16)
 
+    load_tokens = [
+        pltpu.make_async_copy(source, held_tokens.at[batch], loads.at[3 + batch])
+        for batch, source in enumerate((tokens_one, tokens_two))
+    ]
     load_in = pltpu.make_async_copy(w_in, held_in, loads.at[0])
     load_out = pltpu.make_async_copy(w_out, held_out, loads.at[1])
 
     stage_one(0)
+    for load in load_tokens:
+        load.start()
     meet_all()
     place_one, place_two = positions()
+    for load in load_tokens:
+        load.wait()
     fill_outbox(place_one, place_two)
     send_tokens()
     stage_one(1)
@@ -394,13 +402,13 @@
     load_out.wait()
     settle(token_recv.at[0], mailbox.at[pl.ds(0, devices - 1)])
     experts(0)
+    stage_three(1)
     experts(1)
-    stage_three(1)
+    stage_four(0)
     experts(2)
+    stage_four(1)
     experts(3)
     returned[myself] = mailbox[my_slot]
-    stage_four(0)
-    stage_four(1)
     stage_five(0)
     stage_five(1)
     settle(token_recv.at[1], returned.at[pl.ds(0, devices - 1)])
@@ -438,7 +446,7 @@
         out_shape=[jax.ShapeDtypeStruct((tokens_here, width), dtype)] * 2
         + [jax.ShapeDtypeStruct((1, 128), jnp.int32)]
         + [jax.ShapeDtypeStruct((hidden_units, width), dtype)] * 2,
-        in_specs=[vmem] * 8 + [hbm] * 2,
+        in_specs=[hbm] * 2 + [vmem] * 6 + [hbm] * 2,
         out_specs=[vmem] * 3 + [hbm] * 2,
         scratch_shapes=[
             each(LINE, piece, width),
@@ -461,8 +469,9 @@
             pltpu.SemaphoreType.DMA((5, HALVES, 3)),
             pltpu.SemaphoreType.DMA((2,)),
             pltpu.SemaphoreType.DMA((2,)),
-            pltpu.SemaphoreType.DMA((3,)),
+            pltpu.SemaphoreType.DMA((5,)),
             pltpu.SemaphoreType.REGULAR((2,)),
+            pltpu.VMEM((BATCHES, tokens_here, width), dtype),
         ],
         compiler_params=pltpu.CompilerParams(
             collective_id=1 + which, has_side_effects=True, vmem_limit_bytes=60 * 1024 * 1024

time: 189 us -> 189 us (level)
  no operation moved by 1% of the time
where the time goes in v6:
time: 189 us; the launch traced here: 188 us
  Pallas kernels  184 us (97%)
  other arithmetic  2.42 us (1%)
    pallas_call x1, Pallas kernels, layer(): pl.pallas_call(functools.partial(layer_kernel, LIMITS[which]), out_shape=...  176 us
    pallas_call x1, Pallas kernels, keep(): pl.pallas_call(keep_kernel, out_shape=like, in_specs=[pl.BlockSpec(memory...  8.15 us

profile of v6, /device:TPU:1, one launch (start us, length us, event | category | flops | bytes accessed | tf_op | source)
XLA Modules:
  0.0 188.4 jit_solution(15872163004802463093)
XLA Ops:
  0.6 0.8 and_select_fusion.4
  1.4 0.8 fusion
  2.2 0.2 add_reduce_fusion
  2.4 0.7 add_reduce_fusion.2
  3.7 176.3 %conditional.1 = ((bf16[256,768]{1,0:T(8,128)(2,1)S(1)}, bf16[256,768]{1,0:T(8,128)(2,1)S(1)}, s32[1,128]{1,0:T(1,128)S(1)}, bf16[3072,768]{1,0:T(8,128)(2,1)}, bf16[3072,768]{1,0:T(8,128)(2,1)})) conditional(s32[]{:T(128)} %clamp.3, (f32[256]{0:T(256)}, f32[256]{0:T(256)}, s32[256,1]{0,1:T(1,128)}, ...), branch_computations={%region_3.4_spmd, %region_4.5_spmd, %region_5.6_spmd, %region_6.9_... | conditional | flops 4836568064 | bytes 488108480 | solution.py:632
  3.9 175.6 %branch_1_fun.1 = (bf16[256,768]{1,0:T(8,128)(2,1)S(1)}, bf16[256,768]{1,0:T(8,128)(2,1)S(1)}, s32[1,128]{1,0:T(1,128)S(1)}, bf16[3072,768]{1,0:T(8,128)(2,1)}, bf16[3072,768]{1,0:T(8,128)(2,1)}) custom-call(bf16[256,768]{1,0:T(8,128)(2,1)} %get-tuple-element.95.tokens_one, bf16[256,768]{1,0:T(8,128)(2,1)} %get-tuple-element.96.tokens_two, ...), custom_call_target="tpu_custom_call" | custom-call | flops 4831838208 | bytes 400000000 | tf_op jit(solution)/shard_map/cond/branch_1_fun/pallas_call | solution.py:444
  180.1 8.1 %shard_map.129 = (bf16[256,768]{1,0:T(8,128)(2,1)}, bf16[256,768]{1,0:T(8,128)(2,1)}, bf16[1,3072,768]{2,1,0:T(8,128)(2,1)}, bf16[1,3072,768]{2,1,0:T(8,128)(2,1)}) custom-call(s32[1,128]{1,0:T(1,128)S(1)} %get-tuple-element.139.flags, bf16[3072,768]{1,0:T(8,128)(2,1)} %get-tuple-element.140.came_in, bf16[3072,768]{1,0:T(8,128)(2,1)} %get-tuple-element.141.came_out, ...), custom_call_target="tpu_custom_call" | custom-call | tf_op jit(solution)/shard_map/pallas_call | solution.py:546
